TPU v7x, 128 devices: a whole 4x4x4 slice. The times are simulated.
128 devices in a mesh: row: 16 (over z_hi, y, core), col: 8 (over x, z_lo).
Axes of the slice: x: 4, y: 4, z: 4 (z_hi: 2, z_lo: 2; z = z_hi * 2 + z_lo), core: 2. Of those that a mesh axis runs over, the one named last changes fastest.
Arguments:
- image_tokens: bfloat16 [1, 256, 128, 1024], P(None, 'row', 'col'), may hold values from -6 to 6
- qkv_three: bfloat16 [3, 1024, 1024], replicated, may hold values from -0.125 to 0.125, as said below
- proj_three: bfloat16 [1024, 1024], replicated, may hold values from -0.1875 to 0.1875
- scale_three: float32 [32], replicated, may hold values from 1.6 to 5
- table_three: float32 [961, 32], replicated, may hold values from -6 to 6
- gain_three: float32 [1024], replicated, may hold values from 0.25 to 1.75
- merge_weight: bfloat16 [4096, 2048], P(None, 'row'), may hold values from -0.09375 to 0.09375
- merge_gain: float32 [2048], replicated, may hold values from 0.25 to 1.75
- qkv_four: bfloat16 [3, 2048, 2048], P(None, None, 'row'), may hold values from -0.088388348 to 0.088388348, as said below
- proj_four: bfloat16 [2048, 2048], P('row'), may hold values from -0.125 to 0.125
- scale_four: float32 [64], P('row'), may hold values from 1.6 to 5
- table_four: float32 [961, 64], P(None, 'row'), may hold values from -6 to 6
- gain_attend: float32 [2048], replicated, may hold values from 0.25 to 1.75
- expand_weight: bfloat16 [2048, 8192], P(None, 'row'), may hold values from -0.125 to 0.125
- reduce_weight: bfloat16 [8192, 2048], P('row'), may hold values from -0.0625 to 0.0625
- gain_feed: float32 [2048], replicated, may hold values from 0.25 to 1.75
Outputs:
- section_out: bfloat16 [1, 128, 64, 2048], P(None, 'row', 'col')
Inputs may be any that keep to these rules, and one draw needn't show every extreme that they name: `qkv_three`: a projection's entries, about 1024 ** -0.5 in deviation. `qkv_four`: a projection's entries, about 2048 ** -0.5 in deviation.
All inputs are finite; a program needn't handle non-finite values.
Results may differ from a plain program's by a relative error of at most 0.035.
The roundings to bfloat16 on the way count: a program that leaves them out, or rounds other values in their place, can miss the bound.
Values may be sent and summed in bfloat16 or wider, within the bound.
No kernel may reach another device: no remote copies, remote signals or barrier semaphores. Data moves between devices by JAX's collectives and lax.ppermute only.
A program may use at most 192 MiB of HBM per device.

v0:
```python
import functools
import math

import jax
import jax.numpy as jnp
from jax import lax
from jax.experimental import pallas as pl
from jax.experimental.pallas import tpu as pltpu
from jax.sharding import PartitionSpec as P

HD = 32
WIN = 16
TOKENS = WIN * WIN
GROUP = 8
TILE = 64
LANES = 128

EPSILON = 1e-05
FLOOR = 1e-06

ROWS = 16
COLS = 8
VMEM = 24 * 1024 * 1024
MOST = 60 * 1024 * 1024
LOG2E = math.log2(math.e)


def place_of(row, col):
    return row // 8, row // 2 % 4, row % 2, col // 2, col % 2


def flat_of(zh, y, core, x, zl):
    return (zh * 8 + y * 2 + core) * COLS + x * 2 + zl


def permute(value, target):
    pairs = [
        (row * COLS + col, target(row, col)) for row in range(ROWS) for col in range(COLS)
    ]
    return lax.ppermute(value, ("row", "col"), pairs)


def home(row, col):
    zh, y, core, x, zl = place_of(row % ROWS, col % COLS)
    return flat_of(zh ^ zl, y // 2 * 2 + core, y % 2, x, zl)


def unhome(row, col):
    zh, y, core, x, zl = place_of(row, col)
    return flat_of(zh ^ zl, y // 2 * 2 + core, y % 2, x, zl)


MEMBERS = tuple((dy, dz) for dy in range(4) for dz in range(2))
ORDER = ((0, 0), (1, 0), (3, 0), (0, 1), (2, 0), (2, 1), (1, 1), (3, 1))


def onward(row, col, dy, dz):
    zh, y, core, x, zl = place_of(row, col)
    return flat_of(zh ^ dz, (y + dy) % 4, core, x, zl ^ dz)


def send(value, dy, dz):
    return permute(value, functools.partial(onward, dy=dy, dz=dz))


def gather(value):
    side = send(value, 0, 1)
    before, after = send(value, 1, 0), send(value, 3, 0)
    far = send(jnp.concatenate([value, side], axis=0), 2, 0)
    over = send(jnp.concatenate([before, after], axis=0), 0, 1)
    return [value, before, after, side, far, over]


def scatter(lows, highs):
    far = send(highs[1], 0, 1)
    lows = [lows[0], send(lows[1], 1, 0), send(lows[2], 2, 0), send(lows[3], 3, 0)]
    low, low_side = add_up(lows, 2)
    high, *high_far = add_up([highs[0], far], 4)
    low_side = send(low_side, 0, 1)
    high_far = [send(part, dy + 1, 0) for dy, part in enumerate(high_far)]
    return [low, low_side], [high] + high_far


def other_core(value):
    return permute(value, lambda row, col: (row ^ 1) * COLS + col)


def table_rows(table, logit, *flags):
    heads = table.shape[1]
    span = 2 * WIN - 1
    grid = jnp.transpose(16.0 * LOG2E * jax.nn.sigmoid(table)).reshape(heads, span, span)
    scaled = LOG2E * jnp.exp(jnp.minimum(logit, math.log(100.0)))
    extra = [scaled] + [jnp.full((heads,), flag, jnp.float32) for flag in flags]
    extra = jnp.pad(jnp.stack(extra, axis=1), ((0, 0), (0, 32 - len(extra))))
    grid = jnp.pad(grid, ((0, 0), (0, 1), (0, 0)))
    grid = jnp.concatenate([grid, extra[:, :, None]], axis=2).reshape(heads, 8, 4, 32)
    return jnp.transpose(grid, (0, 2, 1, 3)).reshape(heads, 4, 256)


def build_bias(rows, bias_ref):
    lane = lax.broadcasted_iota(jnp.int32, (WIN, 256), 1)
    slot = lane % 32 // 8
    lows = jnp.zeros((WIN, 256), jnp.float32)
    highs = jnp.zeros((WIN, 256), jnp.float32)
    for r in range(4):
        wide = jnp.broadcast_to(rows[r : r + 1], (WIN, 256))
        skew = pltpu.roll(wide, 256 - 15, 1, stride=1, stride_axis=0)
        low = pltpu.roll(skew, 8 * r, 1) if r else skew
        high = pltpu.roll(skew, (8 * r - 8) % 256, 1) if r != 1 else skew
        lows = jnp.where(slot == r, low, lows)
        highs = jnp.where(slot == r, high, highs)
    for c in range(WIN):
        by = (256 - (15 - c) * 8) % 256
        low = pltpu.roll(lows, by, 1) if by else lows
        high = pltpu.roll(highs, by, 1) if by else highs
        for half in range(2):
            at = (half * WIN + c) * 8
            bias_ref[at : at + 8, 0:LANES] = low[half * 8 : half * 8 + 8, 0:LANES]
            bias_ref[at : at + 8, LANES : 2 * LANES] = high[half * 8 : half * 8 + 8, 0:LANES]


def unit_heads(values):
    values = values.astype(jnp.float32)
    parts = []
    for at in range(0, values.shape[0], HD):
        part = values[at : at + HD]
        length = jnp.sqrt(jnp.sum(part * part, axis=0, keepdims=True))
        parts.append((part / jnp.maximum(length, FLOOR)).astype(jnp.bfloat16))
    return jnp.concatenate(parts, axis=0)


def head_attend(queries, keys, values, head, scaled, bias, mask):
    down = lax.broadcasted_iota(jnp.int32, queries.shape, 0) // HD
    own = jnp.where(down == head, queries, jnp.zeros_like(queries))
    scores = jnp.dot(keys, own, preferred_element_type=jnp.float32)
    scores = scores * scaled + bias
    if mask is not None:
        scores = scores + mask
    peak = jnp.max(scores, axis=0, keepdims=True)
    weights = jnp.exp2(scores - peak)
    total = jnp.sum(weights, axis=0, keepdims=True)
    out = jnp.dot(values, weights.astype(jnp.bfloat16), preferred_element_type=jnp.float32)
    return out * (1.0 / total)


def project(x, qkv):
    q, k, v = (
        jnp.dot(x, weight, preferred_element_type=jnp.float32).astype(jnp.bfloat16)
        for weight in qkv
    )
    q = unit_heads(jnp.transpose(q))
    k = jnp.transpose(unit_heads(jnp.transpose(k)))
    return q, k, jnp.transpose(v)


def attend(q, k, v, rows, bias, mask, attended):
    heads = LANES // HD
    for head in range(q.shape[0] // HD):
        at = head // heads * LANES
        build_bias(rows[head], bias.at[head % 2])
        for start in range(0, q.shape[1], TOKENS):
            window = slice(start, start + TOKENS)
            out = head_attend(
                q[at : at + LANES, window],
                k[window, at : at + LANES],
                v[head * HD : (head + 1) * HD, window],
                head % heads,
                rows[head][0:1, 31:32],
                bias[head % 2],
                mask,
            )
            attended[head * HD : (head + 1) * HD, window] = out.astype(jnp.bfloat16)


def norm(values, gain):
    centre = values - jnp.mean(values, axis=-1, keepdims=True)
    spread = jnp.mean(centre * centre, axis=-1, keepdims=True)
    return centre * lax.rsqrt(spread + EPSILON) * gain


def first_kernel(x_ref, qkv_hbm, rows_ref, proj_hbm, gain_ref, *rest):
    outs, (bias, mask, attended, mixed, qkv_ref, proj_ref, arrived) = rest[:4], rest[4:]
    block = attended.shape[0]
    heads = block // HD

    def copies(i):
        at = pl.ds(pl.multiple_of(i * block, block), block)
        return (
            pltpu.make_async_copy(qkv_hbm.at[:, :, at], qkv_ref.at[:, :, at], arrived.at[0, i]),
            pltpu.make_async_copy(proj_hbm.at[at, :], proj_ref.at[at, :], arrived.at[1, i]),
        )

    for i in range(x_ref.shape[1] // block):
        for copy in copies(i):
            copy.start()
    down = lax.broadcasted_iota(jnp.int32, (TOKENS, TOKENS), 0) // TILE
    across = lax.broadcasted_iota(jnp.int32, (TOKENS, TOKENS), 1) // TILE
    apart = jnp.where(down % 2 != across % 2, rows_ref[0][1:2, 31:32], 0.0)
    apart = apart + jnp.where(down // 2 != across // 2, rows_ref[0][2:3, 31:32], 0.0)
    mask[...] = jnp.where(apart > 0, -100.0 * LOG2E, 0.0).astype(jnp.float32)
    mixed[...] = jnp.zeros_like(mixed)
    x = x_ref[...]

    def step(i, _):
        at = pl.ds(pl.multiple_of(i * block, block), block)
        for copy in copies(i):
            copy.wait()
        q, k, v = project(x_ref[...], [qkv_ref[s, :, at] for s in range(3)])
        rows = [rows_ref[i * heads + head] for head in range(heads)]
        attend(q, k, v, rows, bias, mask[...], attended)
        mixed[...] = mixed[...] + jnp.dot(
            jnp.transpose(attended[...]), proj_ref[at, :], preferred_element_type=jnp.float32
        )
        return 0

    lax.fori_loop(0, x.shape[1] // block, step, 0)
    section = (x.astype(jnp.float32) + norm(mixed[...], gain_ref[...])).astype(jnp.bfloat16)
    at = lax.broadcasted_iota(jnp.int32, (TILE, TILE), 0)
    source = at // 4 % 4 * 16 + at // 16 % 2 * 8 + at % 4 * 2 + at // 32
    pick = (lax.broadcasted_iota(jnp.int32, (TILE, TILE), 1) == source).astype(jnp.bfloat16)
    chans = x.shape[1]
    for quadrant in range(4):
        rows = section[quadrant * TILE : (quadrant + 1) * TILE]
        moved = jnp.dot(pick, rows, preferred_element_type=jnp.float32).astype(jnp.bfloat16)
        for part in range(4):
            outs[quadrant][:, part * chans : (part + 1) * chans] = moved[
                part * 16 : (part + 1) * 16
            ]


def first_attention(x, qkv, rows, proj, gain):
    chans = x.shape[1]
    vmem = pl.BlockSpec(memory_space=pltpu.VMEM)
    anywhere = pl.BlockSpec(memory_space=pltpu.HBM)
    return pl.pallas_call(
        first_kernel,
        in_specs=[vmem, anywhere, vmem, anywhere, vmem],
        out_specs=[vmem] * 4,
        out_shape=[jax.ShapeDtypeStruct((16, 4 * chans), jnp.bfloat16)] * 4,
        scratch_shapes=[
            pltpu.VMEM((2, TOKENS, TOKENS), jnp.float32),
            pltpu.VMEM((TOKENS, TOKENS), jnp.float32),
            pltpu.VMEM((2 * LANES, TOKENS), jnp.bfloat16),
            pltpu.VMEM((TOKENS, chans), jnp.float32),
            pltpu.VMEM(qkv.shape, jnp.bfloat16),
            pltpu.VMEM(proj.shape, jnp.bfloat16),
            pltpu.SemaphoreType.DMA((2, chans // (2 * LANES))),
        ],
        compiler_params=pltpu.CompilerParams(vmem_limit_bytes=MOST),
        name="first_attention",
    )(x, qkv, rows, proj, gain)


PIECES = 6


def lay(pieces, whole):
    at = 0
    for piece in pieces:
        rows = piece.shape[0]
        whole[at : at + rows, :] = piece[...]
        at += rows


def fetch(pairs, arrived):
    copies = [
        pltpu.make_async_copy(source, target, arrived.at[i])
        for i, (source, target) in enumerate(pairs)
    ]
    for copy in copies:
        copy.start()
    return copies


def land(copies):
    for copy in copies:
        copy.wait()


def merge_kernel(core_ref, *refs):
    pieces, (own_hbm, other_hbm, out_ref, x, weight, arrived) = (
        refs[:PIECES],
        refs[PIECES:],
    )
    copies = fetch([(own_hbm, weight.at[:, :LANES]), (other_hbm, weight.at[:, LANES:])], arrived)
    lay(pieces, x)
    land(copies)
    both = jnp.dot(x[...], weight[...], preferred_element_type=jnp.float32).astype(jnp.bfloat16)
    own, other = both[:, :LANES], both[:, LANES:]
    first = core_ref[0] == 0
    out_ref[:, :LANES] = jnp.where(first, own, other)
    out_ref[:, LANES:] = jnp.where(first, other, own)


def merge(core, pieces, own, other):
    smem = pl.BlockSpec(memory_space=pltpu.SMEM)
    vmem = pl.BlockSpec(memory_space=pltpu.VMEM)
    tokens = GROUP * TILE
    return pl.pallas_call(
        merge_kernel,
        in_specs=[smem] + [vmem] * PIECES + [pl.BlockSpec(memory_space=pltpu.HBM)] * 2,
        out_specs=vmem,
        out_shape=jax.ShapeDtypeStruct((tokens, 2 * LANES), jnp.bfloat16),
        scratch_shapes=[
            pltpu.VMEM((tokens, pieces[0].shape[1]), jnp.bfloat16),
            pltpu.VMEM((own.shape[0], 2 * LANES), jnp.bfloat16),
            pltpu.SemaphoreType.DMA((2,)),
        ],
        compiler_params=pltpu.CompilerParams(vmem_limit_bytes=MOST - 3 * 1024 * 1024),
        name="merge_patches",
    )(core, *pieces, own, other)


def second_kernel(at_ref, *refs):
    parts, refs = refs[:PIECES], refs[PIECES:]
    qkv_refs, rows_refs, proj_refs, gain_ref = refs[0:2], refs[2:4], refs[4:6], refs[6]
    merged_ref, outs = refs[7], refs[8:14]
    merged, bias, attended, sums, qkv, proj, arrived = refs[14:]
    sides = (slice(0, LANES), slice(LANES, 2 * LANES))
    copies = fetch(
        [(qkv_refs[i], qkv.at[:, :, sides[i]]) for i in range(2)]
        + [(proj_refs[i], proj.at[sides[i], :]) for i in range(2)],
        arrived,
    )
    wide = 2 * LANES
    half = TILE // 2
    whole = GROUP * wide
    for dy, dz, part in ((dy, dz, part) for dy, dz in ORDER for part in range(2)):
        row = pl.multiple_of(at_ref[dy * 2 + dz] * TILE + part * half, half)
        pieces = []
        for fy, fz in MEMBERS:
            index = ORDER.index((fy, fz))
            source, start = (index, 0) if index < 4 else (2 + index // 2, index % 2)
            block = ORDER.index(((dy - fy) % 4, dz ^ fz))
            start = start * GROUP * TILE + block * TILE + part * half
            piece = parts[source][start : start + half, :]
            pieces.append(piece.astype(jnp.float32))
        mean = sum(jnp.sum(piece, axis=-1, keepdims=True) for piece in pieces) / whole
        pieces = [piece - mean for piece in pieces]
        spread = sum(jnp.sum(piece * piece, axis=-1, keepdims=True) for piece in pieces) / whole
        inverse = lax.rsqrt(spread + EPSILON)
        for i, piece in enumerate(pieces):
            col = pl.multiple_of(at_ref[GROUP + i] * wide, wide)
            values = piece * inverse * gain_ref[:, pl.ds(col, wide)]
            merged[pl.ds(row, half), pl.ds(col, wide)] = values.astype(jnp.bfloat16)
    merged_ref[...] = merged[pl.ds(pl.multiple_of(at_ref[0] * TILE, TILE), TILE), :]

    land(copies[:2])
    q, k, v = project(merged[...], [qkv[s] for s in range(3)])
    rows = [rows_refs[side][head] for side in range(2) for head in range(LANES // HD)]
    attend(q, k, v, rows, bias, None, attended)
    land(copies[2:])
    sums[...] = jnp.dot(
        jnp.transpose(attended[...]), proj[...], preferred_element_type=jnp.float32
    ).astype(jnp.bfloat16)
    for dy, dz in MEMBERS:
        place = at_ref[-dy % 4 * 2 + dz]
        values = sums[pl.ds(pl.multiple_of(place * TILE, TILE), TILE), :]
        put_part(outs, dy, dz, 0, 0, sums.shape[1], values)


def second_attention(at, parts, qkv, rows, proj, gain):
    smem = pl.BlockSpec(memory_space=pltpu.SMEM)
    vmem = pl.BlockSpec(memory_space=pltpu.VMEM)
    anywhere = pl.BlockSpec(memory_space=pltpu.HBM)
    chans = gain.shape[1]
    tokens = GROUP * TILE
    tile = jax.ShapeDtypeStruct((TILE, chans), jnp.bfloat16)
    return pl.pallas_call(
        second_kernel,
        in_specs=[smem]
        + [vmem] * PIECES
        + [anywhere] * 2
        + [vmem] * 2
        + [anywhere] * 2
        + [vmem],
        out_specs=[vmem] * 7,
        out_shape=[tile] + part_shapes(chans),
        scratch_shapes=[
            pltpu.VMEM((tokens, chans), jnp.bfloat16),
            pltpu.VMEM((2, TOKENS, TOKENS), jnp.float32),
            pltpu.VMEM((2 * LANES, tokens), jnp.bfloat16),
            pltpu.VMEM((tokens, chans), jnp.bfloat16),
            pltpu.VMEM((3, chans, 2 * LANES), jnp.bfloat16),
            pltpu.VMEM((2 * LANES, chans), jnp.bfloat16),
            pltpu.SemaphoreType.DMA((4,)),
        ],
        compiler_params=pltpu.CompilerParams(vmem_limit_bytes=MOST - 2 * 1024 * 1024),
        name="second_attention",
    )(at, *parts, *qkv, *rows, *proj, gain)


def feed_kernel(*refs):
    pieces, refs = refs[:PIECES], refs[PIECES:]
    outs, (x, hidden, expand, reduce, arrived) = refs[4:10], refs[10:]
    units = expand.shape[2]
    copies = fetch(
        [(refs[side], expand.at[side]) for side in range(2)]
        + [(refs[2 + side], reduce.at[pl.ds(side * units, units)]) for side in range(2)],
        arrived,
    )
    lay(pieces, x)
    for side in range(2):
        land(copies[side : side + 1])
        lifted = jnp.dot(x[...], expand[side][...], preferred_element_type=jnp.float32)
        values = 0.5 * lifted * (1.0 + lax.erf(lifted * math.sqrt(0.5)))
        hidden[:, side * units : (side + 1) * units] = values.astype(jnp.bfloat16)
    block = 4 * LANES
    chans = reduce.shape[1]
    land(copies[2:])
    for start in range(0, chans, block):
        cols = slice(start, start + block)
        total = jnp.dot(hidden[...], reduce[:, cols], preferred_element_type=jnp.float32)
        total = total.astype(jnp.bfloat16)
        for dy, dz in MEMBERS:
            at = ORDER.index((-dy % 4, dz)) * TILE
            put_part(outs, dy, dz, 0, start, chans, total[at : at + TILE])


def feed_forward(pieces, expand, reduce):
    chans, units = expand[0].shape
    tokens = GROUP * TILE
    vmem = pl.BlockSpec(memory_space=pltpu.VMEM)
    shapes = part_shapes(chans)
    return pl.pallas_call(
        feed_kernel,
        in_specs=[vmem] * PIECES + [pl.BlockSpec(memory_space=pltpu.HBM)] * 4,
        out_specs=[vmem] * len(shapes),
        out_shape=shapes,
        scratch_shapes=[
            pltpu.VMEM((tokens, chans), jnp.bfloat16),
            pltpu.VMEM((tokens, 2 * units), jnp.bfloat16),
            pltpu.VMEM((2, chans, units), jnp.bfloat16),
            pltpu.VMEM((2 * units, chans), jnp.bfloat16),
            pltpu.SemaphoreType.DMA((4,)),
        ],
        compiler_params=pltpu.CompilerParams(vmem_limit_bytes=VMEM),
        name="feed_forward",
    )(*pieces, *expand, *reduce)


def add_up(parts, count):
    total = sum(part.astype(jnp.float32) for part in parts).astype(jnp.bfloat16)
    return [total[i * TILE : (i + 1) * TILE] for i in range(count)]


def join_kernel(count, bases, *refs):
    lows, highs, refs = refs[: count[0]], refs[count[0] : sum(count)], refs[sum(count) :]
    base, gain_ref, outs = refs[:bases], refs[bases], refs[bases + 1 :]
    low, high = (sum(part[...].astype(jnp.float32) for part in parts) for parts in (lows, highs))
    total = norm(jnp.concatenate([low, high], axis=1), gain_ref[...])
    base = jnp.concatenate([part[...] for part in base], axis=0)
    total = (base.astype(jnp.float32) + total).astype(jnp.bfloat16)
    at = 0
    for out_ref in outs:
        rows = out_ref.shape[0]
        out_ref[...] = total[at : at + rows]
        at += rows


def join(lows, highs, base, gain, outs):
    vmem = pl.BlockSpec(memory_space=pltpu.VMEM)
    shape = jax.ShapeDtypeStruct((TILE // outs, gain.shape[1]), jnp.bfloat16)
    return pl.pallas_call(
        functools.partial(join_kernel, (len(lows), len(highs)), len(base)),
        in_specs=[vmem] * (len(lows) + len(highs) + len(base) + 1),
        out_specs=[vmem] * outs,
        out_shape=[shape] * outs,
        compiler_params=pltpu.CompilerParams(vmem_limit_bytes=VMEM),
        name="join_sums",
    )(*lows, *highs, *base, gain)


def part_shapes(chans):
    low = jax.ShapeDtypeStruct((2 * TILE, chans // 2), jnp.bfloat16)
    high = jax.ShapeDtypeStruct((4 * TILE, chans // 2), jnp.bfloat16)
    return [low] * 4 + [high] * 2


def put_part(outs, dy, dz, start, col, chans, values):
    rows, wide = values.shape
    middle = chans // 2
    if col < middle:
        at = dz * TILE + start
        low = min(wide, middle - col)
        outs[dy][at : at + rows, col : col + low] = values[:, :low]
    if col + wide > middle:
        at = dy * TILE + start
        skip = max(middle - col, 0)
        outs[4 + dz][at : at + rows, col + skip - middle : col + wide - middle] = values[:, skip:]


def on_device(
    image_tokens,
    qkv_three,
    proj_three,
    scale_three,
    table_three,
    gain_three,
    merge_weight,
    merge_gain,
    qkv_four,
    proj_four,
    scale_four,
    table_four,
    gain_attend,
    expand_weight,
    reduce_weight,
    gain_feed,
):
    chans = image_tokens.shape[3]
    half = WIN // 2
    row = lax.axis_index("row")
    col = lax.axis_index("col")
    zh, y, core, zl = row // 8, row // 2 % 4, row % 2, col % 2

    image = image_tokens[0]
    corner = permute(
        image[:half, :half], lambda r, c: (r - 1) % ROWS * COLS + (c - 1) % COLS
    ).reshape(TILE, chans)
    below = permute(image[:half, half:], lambda r, c: (r - 1) % ROWS * COLS + c).reshape(
        TILE, chans
    )
    beside = permute(image[half:, :half], lambda r, c: r * COLS + (c - 1) % COLS).reshape(
        TILE, chans
    )
    corner_of = image[half:, half:].reshape(TILE, chans)
    ends = ((row == ROWS - 1).astype(jnp.float32), (col == COLS - 1).astype(jnp.float32))
    rows_three = table_rows(table_three, scale_three, *ends)
    corner, below, beside, rows_three = lax.optimization_barrier(
        (corner, below, beside, rows_three)
    )
    x = jnp.concatenate([corner_of, below, beside, corner], axis=0)
    weights = (merge_weight, qkv_four, proj_four, expand_weight, reduce_weight)
    x, weights = lax.optimization_barrier((x, weights))
    merge_weight, qkv_four, proj_four, expand_weight, reduce_weight = weights
    swapped = [other_core(value) for value in weights]
    quadrants = first_attention(x, qkv_three, rows_three, proj_three, gain_three[None])
    quadrants, swapped, table_four = lax.optimization_barrier((quadrants, swapped, table_four))
    merge_other, qkv_other, proj_other, expand_other, reduce_other = swapped

    lower_right = permute(quadrants[0], lambda r, c: home(r, c))
    lower_left = permute(quadrants[2], lambda r, c: home(r, c + 1))
    upper_right = permute(quadrants[1], lambda r, c: home(r + 1, c))
    upper_left = permute(quadrants[3], lambda r, c: home(r + 1, c + 1))
    halves = (
        jnp.concatenate([left.reshape(4, 4, -1), right.reshape(4, 4, -1)], axis=1)
        for left, right in ((upper_left, upper_right), (lower_left, lower_right))
    )
    tile = jnp.concatenate(list(halves), axis=0).reshape(TILE, -1)
    rows_four = table_rows(table_four, scale_four)
    rows_other = other_core(rows_four)
    reduced = merge(core[None].astype(jnp.int32), gather(tile), merge_weight, merge_other)

    dy = jnp.arange(GROUP, dtype=jnp.int32) // 2
    dz = jnp.arange(GROUP, dtype=jnp.int32) % 2
    far = (y - dy) % 4
    place = far // 2 * 4 + (zl ^ dz) * 2 + far % 2
    channel = (zh ^ dz) * 4 + far
    at = jnp.concatenate([place, channel]).astype(jnp.int32)
    merged, *parts = second_attention(
        at,
        gather(reduced),
        (qkv_four, qkv_other),
        (rows_four, rows_other),
        (proj_four, proj_other),
        merge_gain[None],
    )
    after = join(*scatter(parts[:4], parts[4:]), [merged], gain_attend[None], 1)

    parts = feed_forward(
        gather(*after),
        (expand_weight, expand_other),
        (reduce_weight, reduce_other),
    )
    (out,) = join(*scatter(parts[:4], parts[4:]), after, gain_feed[None], 1)
    out = permute(out, unhome)
    return out.reshape(1, half, half, out.shape[1])


def solution(mesh):
    in_specs = (
        P(None, "row", "col", None),
        P(),
        P(),
        P(),
        P(),
        P(),
        P(None, "row"),
        P(),
        P(None, None, "row"),
        P("row", None),
        P("row"),
        P(None, "row"),
        P(),
        P(None, "row"),
        P("row", None),
        P(),
    )
    out_specs = P(None, "row", "col", None)
    return jax.shard_map(
        on_device, mesh=mesh, in_specs=in_specs, out_specs=out_specs, check_vma=False
    )
```

profile of v0, /device:TPU:32, one launch (start us, length us, event | category | flops | bytes accessed | tf_op | source)
XLA Modules:
  0.0 245.4 jit_solution(3918196809663852706)
XLA Ops:
  1.8 3.8 %collective-permute-start = (bf16[8,8,1024]{2,1,0:T(8,128)(2,1)}, bf16[8,8,1024]{2,1,0:T(8,128)(2,1)S(1)}, u32[]{:S(2)}, u32[]{:S(2)}) collective-permute-start(bf16[8,8,1024]{2,1,0:T(8,128)(2,1)} %get-tuple-element.90), channel_id=1, source_target_pairs={{0,127},{1,120},{2,121},{3,122},{4,123},{5,124},{6,125},{7,126},{8... | collective-permute-start | bytes 393224 | tf_op jit(solution)/shard_map/ppermute | solution.py:40
  7.4 4.4 %collective-permute-start.2 = (bf16[8,8,1024]{2,1,0:T(8,128)(2,1)S(1)}, bf16[8,8,1024]{2,1,0:T(8,128)(2,1)}, u32[]{:S(2)}, u32[]{:S(2)}) collective-permute-start(bf16[8,8,1024]{2,1,0:T(8,128)(2,1)S(1)} %get-tuple-element.88), channel_id=1, source_target_pairs={{0,7},{1,0},{2,1},{3,2},{4,3},{5,4},{6,5},{7,6},{8,15},{9,8},{10,9... | collective-permute-start | bytes 393224 | tf_op jit(solution)/shard_map/ppermute | solution.py:40
  19.4 18.2 %first_attention.1 = (bf16[16,4096]{1,0:T(8,128)(2,1)}, bf16[16,4096]{1,0:T(8,128)(2,1)}, bf16[16,4096]{1,0:T(8,128)(2,1)}, bf16[16,4096]{1,0:T(8,128)(2,1)}) custom-call(bf16[256,1024]{1,0:T(8,128)(2,1)} %pad_maximum_fusion.2.x_ref, bf16[3,1024,1024]{2,1,0:T(8,128)(2,1)} %qkv_hbm.1, f32[32,4,256]{2,1,0:T(4,128)} %reshape.55.rows_ref, ...), custom_call_target="tpu_custom_call" | custom-call | tf_op jit(solution)/shard_map/first_attention/pallas_call | solution.py:235
  48.9 4.2 %collective-permute-done.11 = bf16[16,4096]{1,0:T(8,128)(2,1)S(1)} collective-permute-done((bf16[16,4096]{1,0:T(8,128)(2,1)}, bf16[16,4096]{1,0:T(8,128)(2,1)S(1)}, u32[]{:S(2)}, u32[]{:S(2)}) %collective-permute-start.11) | collective-permute-done | bytes 131104 | tf_op jit(solution)/shard_map/ppermute | solution.py:40
  56.7 12.5 %collective-permute-done.12.refs_1_ = bf16[64,4096]{1,0:T(8,128)(2,1)S(1)} collective-permute-done((bf16[64,4096]{1,0:T(8,128)(2,1)S(1)}, bf16[64,4096]{1,0:T(8,128)(2,1)S(1)}, u32[]{:S(2)}, u32[]{:S(2)}) %collective-permute-start.12) | collective-permute-done | bytes 524320 | tf_op jit(solution)/shard_map/ppermute | solution.py:40
  74.5 19.9 %collective-permute-done.16.refs_5_ = bf16[128,4096]{1,0:T(8,128)(2,1)} collective-permute-done((bf16[128,4096]{1,0:T(8,128)(2,1)S(1)}, bf16[128,4096]{1,0:T(8,128)(2,1)}, u32[]{:S(2)}, u32[]{:S(2)}) %collective-permute-start.16) | collective-permute-done | bytes 1048608 | tf_op jit(solution)/shard_map/ppermute | solution.py:40
  94.4 4.8 %collective-permute-done.15.refs_4_ = bf16[128,4096]{1,0:T(8,128)(2,1)} collective-permute-done((bf16[128,4096]{1,0:T(8,128)(2,1)}, bf16[128,4096]{1,0:T(8,128)(2,1)}, u32[]{:S(2)}, u32[]{:S(2)}) %collective-permute-start.15) | collective-permute-done | bytes 1048608 | tf_op jit(solution)/shard_map/ppermute | solution.py:40
  99.3 5.7 %merge_patches.1.refs_0_ = bf16[512,256]{1,0:T(8,128)(2,1)} custom-call(s32[1]{0:T(128)} %bitcast.core_ref, bf16[64,4096]{1,0:T(8,128)(2,1)} %copy-done.5, bf16[64,4096]{1,0:T(8,128)(2,1)} %copy-done.6, bf16[64,4096]{1,0:T(8,128)(2,1)} %copy-done.7, bf16[64,4096]{1,0:T(8,128)(2,1)} %copy-done.8, bf16[128,4096]{1,0:T(8,128)(2,1)} %collective-permute-done.15.refs_4_, ...), custom_call_target="tpu_custom_call" | custom-call | tf_op jit(solution)/shard_map/merge_patches/pallas_call | solution.py:299
  109.5 3.7 %collective-permute-done.17.refs_1_ = bf16[512,256]{1,0:T(8,128)(2,1)S(1)} collective-permute-done((bf16[512,256]{1,0:T(8,128)(2,1)}, bf16[512,256]{1,0:T(8,128)(2,1)S(1)}, u32[]{:S(2)}, u32[]{:S(2)}) %collective-permute-start.17) | collective-permute-done | bytes 262176 | tf_op jit(solution)/shard_map/ppermute | solution.py:40
  122.0 4.1 %collective-permute-done.21.refs_5_ = bf16[1024,256]{1,0:T(8,128)(2,1)S(1)} collective-permute-done((bf16[1024,256]{1,0:T(8,128)(2,1)}, bf16[1024,256]{1,0:T(8,128)(2,1)S(1)}, u32[]{:S(2)}, u32[]{:S(2)}) %collective-permute-start.21) | collective-permute-done | bytes 524320 | tf_op jit(solution)/shard_map/ppermute | solution.py:40
  126.1 4.0 %collective-permute-done.20.refs_4_ = bf16[1024,256]{1,0:T(8,128)(2,1)} collective-permute-done((bf16[1024,256]{1,0:T(8,128)(2,1)}, bf16[1024,256]{1,0:T(8,128)(2,1)}, u32[]{:S(2)}, u32[]{:S(2)}) %collective-permute-start.20) | collective-permute-done | bytes 524320 | tf_op jit(solution)/shard_map/ppermute | solution.py:40
  130.2 14.1 %second_attention.1 = (bf16[64,2048]{1,0:T(8,128)(2,1)}, bf16[128,1024]{1,0:T(8,128)(2,1)}, bf16[128,1024]{1,0:T(8,128)(2,1)}, bf16[128,1024]{1,0:T(8,128)(2,1)}...) custom-call(s32[16]{0:T(128)} %pad_add_fusion.at_ref, ...), custom_call_target="tpu_custom_call" | custom-call | tf_op jit(solution)/shard_map/second_attention/pallas_call | solution.py:369
  150.3 3.7 %collective-permute-done.23 = bf16[128,1024]{1,0:T(8,128)(2,1)S(1)} collective-permute-done((bf16[128,1024]{1,0:T(8,128)(2,1)}, bf16[128,1024]{1,0:T(8,128)(2,1)S(1)}, u32[]{:S(2)}, u32[]{:S(2)}) %collective-permute-start.23) | collective-permute-done | bytes 262176 | tf_op jit(solution)/shard_map/ppermute | solution.py:40
  164.6 3.8 %collective-permute-done.28.refs_3_ = bf16[64,1024]{1,0:T(8,128)(2,1)S(1)} collective-permute-done((bf16[64,1024]{1,0:T(8,128)(2,1)S(1)}, bf16[64,1024]{1,0:T(8,128)(2,1)S(1)}, u32[]{:S(2)}, u32[]{:S(2)}) %collective-permute-start.28) | collective-permute-done | bytes 131104 | tf_op jit(solution)/shard_map/ppermute | solution.py:40
  175.5 3.6 %collective-permute-done.31.refs_1_ = bf16[64,2048]{1,0:T(8,128)(2,1)S(1)} collective-permute-done((bf16[64,2048]{1,0:T(8,128)(2,1)S(1)}, bf16[64,2048]{1,0:T(8,128)(2,1)S(1)}, u32[]{:S(2)}, u32[]{:S(2)}) %collective-permute-start.31) | collective-permute-done | bytes 262176 | tf_op jit(solution)/shard_map/ppermute | solution.py:40
  179.1 4.1 %collective-permute-done.32.refs_2_ = bf16[64,2048]{1,0:T(8,128)(2,1)S(1)} collective-permute-done((bf16[64,2048]{1,0:T(8,128)(2,1)S(1)}, bf16[64,2048]{1,0:T(8,128)(2,1)S(1)}, u32[]{:S(2)}, u32[]{:S(2)}) %collective-permute-start.32) | collective-permute-done | bytes 262176 | tf_op jit(solution)/shard_map/ppermute | solution.py:40
  185.3 7.1 %collective-permute-done.35.refs_5_ = bf16[128,2048]{1,0:T(8,128)(2,1)S(1)} collective-permute-done((bf16[128,2048]{1,0:T(8,128)(2,1)S(1)}, bf16[128,2048]{1,0:T(8,128)(2,1)S(1)}, u32[]{:S(2)}, u32[]{:S(2)}) %collective-permute-start.35) | collective-permute-done | bytes 524320 | tf_op jit(solution)/shard_map/ppermute | solution.py:40
  192.5 6.1 %collective-permute-done.34.refs_4_ = bf16[128,2048]{1,0:T(8,128)(2,1)S(1)} collective-permute-done((bf16[128,2048]{1,0:T(8,128)(2,1)S(1)}, bf16[128,2048]{1,0:T(8,128)(2,1)S(1)}, u32[]{:S(2)}, u32[]{:S(2)}) %collective-permute-start.34) | collective-permute-done | bytes 524320 | tf_op jit(solution)/shard_map/ppermute | solution.py:40
  198.5 5.4 %feed_forward.1 = (bf16[128,1024]{1,0:T(8,128)(2,1)S(1)}, bf16[128,1024]{1,0:T(8,128)(2,1)S(1)}, bf16[128,1024]{1,0:T(8,128)(2,1)S(1)}, bf16[128,1024]{1,0:T(8,1...) custom-call(bf16[64,2048]{1,0:T(8,128)(2,1)S(1)} %join_sums.2.refs_0_.refs_6_, ...), custom_call_target="tpu_custom_call" | custom-call | tf_op jit(solution)/shard_map/feed_forward/pallas_call | solution.py:425
  204.9 4.6 %collective-permute-start.37 = (bf16[128,1024]{1,0:T(8,128)(2,1)S(1)}, bf16[128,1024]{1,0:T(8,128)(2,1)S(1)}, u32[]{:S(2)}, u32[]{:S(2)}) collective-permute-start(bf16[128,1024]{1,0:T(8,128)(2,1)S(1)} %get-tuple-element.75), channel_id=1, source_target_pairs={{0,32},{1,33},{2,34},{3,35},{4,36},{5,37},{6,38},{7,39},{8,40},{9,... | collective-permute-start | bytes 786440 | tf_op jit(solution)/shard_map/ppermute | solution.py:40
  209.5 3.9 %collective-permute-done.36 = bf16[128,1024]{1,0:T(8,128)(2,1)S(1)} collective-permute-done((bf16[128,1024]{1,0:T(8,128)(2,1)S(1)}, bf16[128,1024]{1,0:T(8,128)(2,1)S(1)}, u32[]{:S(2)}, u32[]{:S(2)}) %collective-permute-start.36) | collective-permute-done | bytes 262176 | tf_op jit(solution)/shard_map/ppermute | solution.py:40
  213.4 3.3 %collective-permute-done.37 = bf16[128,1024]{1,0:T(8,128)(2,1)S(1)} collective-permute-done((bf16[128,1024]{1,0:T(8,128)(2,1)S(1)}, bf16[128,1024]{1,0:T(8,128)(2,1)S(1)}, u32[]{:S(2)}, u32[]{:S(2)}) %collective-permute-start.37) | collective-permute-done | bytes 262176 | tf_op jit(solution)/shard_map/ppermute | solution.py:40
  227.8 9.8 %collective-permute-start.44 = (bf16[64,2048]{1,0:T(8,128)(2,1)S(1)}, bf16[64,2048]{1,0:T(8,128)(2,1)S(1)}, u32[]{:S(2)}, u32[]{:S(2)}) collective-permute-start(bf16[64,2048]{1,0:T(8,128)(2,1)S(1)} %join_sums.3), channel_id=1, source_target_pairs={{0,0},{1,65},{2,2},{3,67},{4,4},{5,69},{6,6},{7,71},{8,16},{9,81},... | collective-permute-start | bytes 786440 | tf_op jit(solution)/shard_map/ppermute | solution.py:40
  237.6 7.1 %collective-permute-done.44 = bf16[64,2048]{1,0:T(8,128)(2,1)S(1)} collective-permute-done((bf16[64,2048]{1,0:T(8,128)(2,1)S(1)}, bf16[64,2048]{1,0:T(8,128)(2,1)S(1)}, u32[]{:S(2)}, u32[]{:S(2)}) %collective-permute-start.44) | collective-permute-done | bytes 262176 | tf_op jit(solution)/shard_map/ppermute | solution.py:40
  (155 shorter events, 83.3 us)
Async XLA Ops:
  1.8 14.7 %collective-permute-start = (bf16[8,8,1024]{2,1,0:T(8,128)(2,1)}, bf16[8,8,1024]{2,1,0:T(8,128)(2,1)S(1)}, u32[]{:S(2)}, u32[]{:S(2)}) collective-permute-start(bf16[8,8,1024]{2,1,0:T(8,128)(2,1)} %get-tuple-element.90), channel_id=1, source_target_pairs={{0,127},{1,120},{2,121},{3,122},{4,123},{5,124},{6,125},{7,126},{8... | collective-permute-start | bytes 393224 | tf_op jit(solution)/shard_map/ppermute | solution.py:40
  5.6 10.9 %collective-permute-start.1 = (bf16[8,8,1024]{2,1,0:T(8,128)(2,1)}, bf16[8,8,1024]{2,1,0:T(8,128)(2,1)}, u32[]{:S(2)}, u32[]{:S(2)}) collective-permute-start(bf16[8,8,1024]{2,1,0:T(8,128)(2,1)} %get-tuple-element.89), channel_id=1, source_target_pairs={{0,120},{1,121},{2,122},{3,123},{4,124},{5,125},{6,126},{7,127},{8... | collective-permute-start | bytes 393224 | tf_op jit(solution)/shard_map/ppermute | solution.py:40
  18.4 19.2 %collective-permute-start.6 = (bf16[2048,512]{1,0:T(8,128)(2,1)S(1)}, bf16[2048,512]{1,0:T(8,128)(2,1)}, u32[]{:S(2)}, u32[]{:S(2)}) collective-permute-start(bf16[2048,512]{1,0:T(8,128)(2,1)S(1)} %copy-done), channel_id=1, source_target_pairs={{0,8},{1,9},{2,10},{3,11},{4,12},{5,13},{6,14},{7,15},{8,0},{9,1},... | collective-permute-start | bytes 6291464 | tf_op jit(solution)/shard_map/ppermute | solution.py:40
  18.4 20.4 %collective-permute-start.7 = (bf16[512,2048]{1,0:T(8,128)(2,1)}, bf16[512,2048]{1,0:T(8,128)(2,1)}, u32[]{:S(2)}, u32[]{:S(2)}) collective-permute-start(bf16[512,2048]{1,0:T(8,128)(2,1)} %refs_8_), channel_id=1, source_target_pairs={{0,8},{1,9},{2,10},{3,11},{4,12},{5,13},{6,14},{7,15},{8,0},{9,1},... | collective-permute-start | bytes 6291464 | tf_op jit(solution)/shard_map/ppermute | solution.py:40
  18.9 18.7 %collective-permute-start.4 = (bf16[3,2048,128]{2,1,0:T(8,128)(2,1)}, bf16[3,2048,128]{2,1,0:T(8,128)(2,1)S(1)}, u32[]{:S(2)}, u32[]{:S(2)}) collective-permute-start(bf16[3,2048,128]{2,1,0:T(8,128)(2,1)} %refs_6_.1), channel_id=1, source_target_pairs={{0,8},{1,9},{2,10},{3,11},{4,12},{5,13},{6,14},{7,15},{8,0},{9,1},... | collective-permute-start | bytes 4718600 | tf_op jit(solution)/shard_map/ppermute | solution.py:40
  18.9 18.7 %collective-permute-start.3 = (bf16[4096,128]{1,0:T(8,128)(2,1)}, bf16[4096,128]{1,0:T(8,128)(2,1)}, u32[]{:S(2)}, u32[]{:S(2)}) collective-permute-start(bf16[4096,128]{1,0:T(8,128)(2,1)} %refs_6_), channel_id=1, source_target_pairs={{0,8},{1,9},{2,10},{3,11},{4,12},{5,13},{6,14},{7,15},{8,0},{9,1},... | collective-permute-start | bytes 3145736 | tf_op jit(solution)/shard_map/ppermute | solution.py:40
  19.4 18.2 %collective-permute-start.5 = (bf16[128,2048]{1,0:T(8,128)(2,1)}, bf16[128,2048]{1,0:T(8,128)(2,1)}, u32[]{:S(2)}, u32[]{:S(2)}) collective-permute-start(bf16[128,2048]{1,0:T(8,128)(2,1)} %refs_10_), channel_id=1, source_target_pairs={{0,8},{1,9},{2,10},{3,11},{4,12},{5,13},{6,14},{7,15},{8,0},{9,1},... | collective-permute-start | bytes 1572872 | tf_op jit(solution)/shard_map/ppermute | solution.py:40
  43.1 10.0 %collective-permute-start.11 = (bf16[16,4096]{1,0:T(8,128)(2,1)}, bf16[16,4096]{1,0:T(8,128)(2,1)S(1)}, u32[]{:S(2)}, u32[]{:S(2)}) collective-permute-start(bf16[16,4096]{1,0:T(8,128)(2,1)} %get-tuple-element.59), channel_id=1, source_target_pairs={{0,0},{1,65},{2,2},{3,67},{4,4},{5,69},{6,6},{7,71},{8,16},{9,81},... | collective-permute-start | bytes 393224 | tf_op jit(solution)/shard_map/ppermute | solution.py:40
  53.4 15.8 %collective-permute-start.12 = (bf16[64,4096]{1,0:T(8,128)(2,1)S(1)}, bf16[64,4096]{1,0:T(8,128)(2,1)S(1)}, u32[]{:S(2)}, u32[]{:S(2)}) collective-permute-start(bf16[64,4096]{1,0:T(8,128)(2,1)S(1)} %maximum_bitcast_fusion.1.refs_0_), channel_id=1, source_target_pairs={{0,16},{1,17},{2,18},{3,19},{4,20},{5,21},{6,22},{7,23},{8,24},{9,... | collective-permute-start | bytes 1572872 | tf_op jit(solution)/shard_map/ppermute | solution.py:40
  54.0 15.3 %collective-permute-start.13 = (bf16[64,4096]{1,0:T(8,128)(2,1)S(1)}, bf16[64,4096]{1,0:T(8,128)(2,1)S(1)}, u32[]{:S(2)}, u32[]{:S(2)}) collective-permute-start(bf16[64,4096]{1,0:T(8,128)(2,1)S(1)} %maximum_bitcast_fusion.1.refs_0_), channel_id=1, source_target_pairs={{0,48},{1,49},{2,50},{3,51},{4,52},{5,53},{6,54},{7,55},{8,56},{9,... | collective-permute-start | bytes 1572872 | tf_op jit(solution)/shard_map/ppermute | solution.py:40
  56.7 14.1 %collective-permute-start.14 = (bf16[64,4096]{1,0:T(8,128)(2,1)S(1)}, bf16[64,4096]{1,0:T(8,128)(2,1)S(1)}, u32[]{:S(2)}, u32[]{:S(2)}) collective-permute-start(bf16[64,4096]{1,0:T(8,128)(2,1)S(1)} %maximum_bitcast_fusion.1.refs_0_), channel_id=1, source_target_pairs={{0,65},{1,64},{2,67},{3,66},{4,69},{5,68},{6,71},{7,70},{8,73},{9,... | collective-permute-start | bytes 1572872 | tf_op jit(solution)/shard_map/ppermute | solution.py:40
  69.3 25.1 %collective-permute-start.16 = (bf16[128,4096]{1,0:T(8,128)(2,1)S(1)}, bf16[128,4096]{1,0:T(8,128)(2,1)}, u32[]{:S(2)}, u32[]{:S(2)}) collective-permute-start(bf16[128,4096]{1,0:T(8,128)(2,1)S(1)} %pad_maximum_fusion.1), channel_id=1, source_target_pairs={{0,65},{1,64},{2,67},{3,66},{4,69},{5,68},{6,71},{7,70},{8,73},{9,... | collective-permute-start | bytes 3145736 | tf_op jit(solution)/shard_map/ppermute | solution.py:40
  72.7 26.6 %collective-permute-start.15 = (bf16[128,4096]{1,0:T(8,128)(2,1)}, bf16[128,4096]{1,0:T(8,128)(2,1)}, u32[]{:S(2)}, u32[]{:S(2)}) collective-permute-start(bf16[128,4096]{1,0:T(8,128)(2,1)} %pad_maximum_fusion), channel_id=1, source_target_pairs={{0,32},{1,33},{2,34},{3,35},{4,36},{5,37},{6,38},{7,39},{8,40},{9,... | collective-permute-start | bytes 3145736 | tf_op jit(solution)/shard_map/ppermute | solution.py:40
  114.1 12.0 %collective-permute-start.21 = (bf16[1024,256]{1,0:T(8,128)(2,1)}, bf16[1024,256]{1,0:T(8,128)(2,1)S(1)}, u32[]{:S(2)}, u32[]{:S(2)}) collective-permute-start(bf16[1024,256]{1,0:T(8,128)(2,1)} %pad_maximum_fusion.4), channel_id=1, source_target_pairs={{0,65},{1,64},{2,67},{3,66},{4,69},{5,68},{6,71},{7,70},{8,73},{9,... | collective-permute-start | bytes 1572872 | tf_op jit(solution)/shard_map/ppermute | solution.py:40
  117.1 13.0 %collective-permute-start.20 = (bf16[1024,256]{1,0:T(8,128)(2,1)}, bf16[1024,256]{1,0:T(8,128)(2,1)}, u32[]{:S(2)}, u32[]{:S(2)}) collective-permute-start(bf16[1024,256]{1,0:T(8,128)(2,1)} %pad_maximum_fusion.3), channel_id=1, source_target_pairs={{0,32},{1,33},{2,34},{3,35},{4,36},{5,37},{6,38},{7,39},{8,40},{9,... | collective-permute-start | bytes 1572872 | tf_op jit(solution)/shard_map/ppermute | solution.py:40
  144.3 9.7 %collective-permute-start.23 = (bf16[128,1024]{1,0:T(8,128)(2,1)}, bf16[128,1024]{1,0:T(8,128)(2,1)S(1)}, u32[]{:S(2)}, u32[]{:S(2)}) collective-permute-start(bf16[128,1024]{1,0:T(8,128)(2,1)} %get-tuple-element.65), channel_id=1, source_target_pairs={{0,16},{1,17},{2,18},{3,19},{4,20},{5,21},{6,22},{7,23},{8,24},{9,... | collective-permute-start | bytes 786440 | tf_op jit(solution)/shard_map/ppermute | solution.py:40
  145.5 11.3 %collective-permute-start.24 = (bf16[128,1024]{1,0:T(8,128)(2,1)}, bf16[128,1024]{1,0:T(8,128)(2,1)S(1)}, u32[]{:S(2)}, u32[]{:S(2)}) collective-permute-start(bf16[128,1024]{1,0:T(8,128)(2,1)} %get-tuple-element.66), channel_id=1, source_target_pairs={{0,32},{1,33},{2,34},{3,35},{4,36},{5,37},{6,38},{7,39},{8,40},{9,... | collective-permute-start | bytes 786440 | tf_op jit(solution)/shard_map/ppermute | solution.py:40
  149.3 10.8 %collective-permute-start.27 = (bf16[256,1024]{1,0:T(8,128)(2,1)}, bf16[256,1024]{1,0:T(8,128)(2,1)S(1)}, u32[]{:S(2)}, u32[]{:S(2)}) collective-permute-start(bf16[256,1024]{1,0:T(8,128)(2,1)} %get-tuple-element.69), channel_id=1, source_target_pairs={{0,65},{1,64},{2,67},{3,66},{4,69},{5,68},{6,71},{7,70},{8,73},{9,... | collective-permute-start | bytes 1572872 | tf_op jit(solution)/shard_map/ppermute | solution.py:40
  171.3 11.9 %collective-permute-start.32 = (bf16[64,2048]{1,0:T(8,128)(2,1)S(1)}, bf16[64,2048]{1,0:T(8,128)(2,1)S(1)}, u32[]{:S(2)}, u32[]{:S(2)}) collective-permute-start(bf16[64,2048]{1,0:T(8,128)(2,1)S(1)} %join_sums.2.refs_0_.refs_6_), channel_id=1, source_target_pairs={{0,48},{1,49},{2,50},{3,51},{4,52},{5,53},{6,54},{7,55},{8,56},{9,... | collective-permute-start | bytes 786440 | tf_op jit(solution)/shard_map/ppermute | solution.py:40
  173.6 11.6 %collective-permute-start.33 = (bf16[64,2048]{1,0:T(8,128)(2,1)S(1)}, bf16[64,2048]{1,0:T(8,128)(2,1)S(1)}, u32[]{:S(2)}, u32[]{:S(2)}) collective-permute-start(bf16[64,2048]{1,0:T(8,128)(2,1)S(1)} %join_sums.2.refs_0_.refs_6_), channel_id=1, source_target_pairs={{0,65},{1,64},{2,67},{3,66},{4,69},{5,68},{6,71},{7,70},{8,73},{9,... | collective-permute-start | bytes 786440 | tf_op jit(solution)/shard_map/ppermute | solution.py:40
  185.2 13.3 %collective-permute-start.34 = (bf16[128,2048]{1,0:T(8,128)(2,1)S(1)}, bf16[128,2048]{1,0:T(8,128)(2,1)S(1)}, u32[]{:S(2)}, u32[]{:S(2)}) collective-permute-start(bf16[128,2048]{1,0:T(8,128)(2,1)S(1)} %pad_maximum_fusion.5), channel_id=1, source_target_pairs={{0,32},{1,33},{2,34},{3,35},{4,36},{5,37},{6,38},{7,39},{8,40},{9,... | collective-permute-start | bytes 1572872 | tf_op jit(solution)/shard_map/ppermute | solution.py:40
  203.9 9.4 %collective-permute-start.36 = (bf16[128,1024]{1,0:T(8,128)(2,1)S(1)}, bf16[128,1024]{1,0:T(8,128)(2,1)S(1)}, u32[]{:S(2)}, u32[]{:S(2)}) collective-permute-start(bf16[128,1024]{1,0:T(8,128)(2,1)S(1)} %get-tuple-element.74), channel_id=1, source_target_pairs={{0,16},{1,17},{2,18},{3,19},{4,20},{5,21},{6,22},{7,23},{8,24},{9,... | collective-permute-start | bytes 786440 | tf_op jit(solution)/shard_map/ppermute | solution.py:40
  204.9 11.7 %collective-permute-start.37 = (bf16[128,1024]{1,0:T(8,128)(2,1)S(1)}, bf16[128,1024]{1,0:T(8,128)(2,1)S(1)}, u32[]{:S(2)}, u32[]{:S(2)}) collective-permute-start(bf16[128,1024]{1,0:T(8,128)(2,1)S(1)} %get-tuple-element.75), channel_id=1, source_target_pairs={{0,32},{1,33},{2,34},{3,35},{4,36},{5,37},{6,38},{7,39},{8,40},{9,... | collective-permute-start | bytes 786440 | tf_op jit(solution)/shard_map/ppermute | solution.py:40
  227.8 16.9 %collective-permute-start.44 = (bf16[64,2048]{1,0:T(8,128)(2,1)S(1)}, bf16[64,2048]{1,0:T(8,128)(2,1)S(1)}, u32[]{:S(2)}, u32[]{:S(2)}) collective-permute-start(bf16[64,2048]{1,0:T(8,128)(2,1)S(1)} %join_sums.3), channel_id=1, source_target_pairs={{0,0},{1,65},{2,2},{3,67},{4,4},{5,69},{6,6},{7,71},{8,16},{9,81},... | collective-permute-start | bytes 786440 | tf_op jit(solution)/shard_map/ppermute | solution.py:40
  (40 other events, 371.2 us)
where the time goes:
time: 249 us; the launch traced here: 245 us
  waiting for transfers between devices  111 us (45%)
  starting transfers between devices  70 us (28%)
  Pallas kernels  44 us (18%)
  other arithmetic  11.7 us (5%)
  local copies, waits for them, and re-layouts  8.37 us (3%)
    ppermute x45, waiting for transfers between devices, permute(): return lax.ppermute(value, ('row', 'col'), pairs)  111 us
    ppermute x45, starting transfers between devices, permute(): return lax.ppermute(value, ('row', 'col'), pairs)  70 us
    pallas_call x1, Pallas kernels, first_attention(): pl.pallas_call(first_kernel, in_specs=[vmem, anywhere, vmem, anywhere, vm...  18.2 us
    pallas_call x1, Pallas kernels, second_attention(): pl.pallas_call(second_kernel, in_specs=[smem] + [vmem] * PIECES + [anywhe...  14.1 us
    pallas_call x1, Pallas kernels, merge(): pl.pallas_call(merge_kernel, in_specs=[smem] + [vmem] * PIECES + [pl.Bloc...  5.7 us
    pallas_call x1, Pallas kernels, feed_forward(): pl.pallas_call(feed_kernel, in_specs=[vmem] * PIECES + [pl.BlockSpec(memo...  5.38 us
  transfers between devices with their start and end apart: 45, of which 27 were waited for; matrix products, arithmetic and copies ran while one was open for 5% of the time, Pallas kernels for 7%

commit v1 on v0

--- a/solution.py
+++ b/solution.py
@@ -63,22 +63,30 @@
     return permute(value, functools.partial(onward, dy=dy, dz=dz))
 
 
-def gather(value):
+def gather(value, steps=False):
     side = send(value, 0, 1)
     before, after = send(value, 1, 0), send(value, 3, 0)
-    far = send(jnp.concatenate([value, side], axis=0), 2, 0)
+    if steps:
+        half = value.shape[0] // 2
+        far = [send(before[:half], 1, 0), send(after[half:], 3, 0)]
+    else:
+        far = [send(value, 2, 0)]
     over = send(jnp.concatenate([before, after], axis=0), 0, 1)
-    return [value, before, after, side, far, over]
-
-
-def scatter(lows, highs):
-    far = send(highs[1], 0, 1)
-    lows = [lows[0], send(lows[1], 1, 0), send(lows[2], 2, 0), send(lows[3], 3, 0)]
-    low, low_side = add_up(lows, 2)
-    high, *high_far = add_up([highs[0], far], 4)
-    low_side = send(low_side, 0, 1)
-    high_far = [send(part, dy + 1, 0) for dy, part in enumerate(high_far)]
-    return [low, low_side], [high] + high_far
+    return [value, before, after, side, *far, send(side, 2, 0), over]
+
+
+def scatter(parts):
+    own, ahead, behind, side, far, over = parts
+    far = send(far, 2, 0)
+    over = send(over, 0, 1)
+    ahead = send(add(ahead, over[:TILE]), 1, 0)
+    behind = send(add(behind, over[TILE:]), 3, 0)
+    side = send(add(side, far[TILE:]), 0, 1)
+    return [own, far, ahead, behind, side]
+
+
+def add(one, other):
+    return (one.astype(jnp.float32) + other.astype(jnp.float32)).astype(jnp.bfloat16)
 
 
 def other_core(value):
@@ -178,8 +186,9 @@
     return centre * lax.rsqrt(spread + EPSILON) * gain
 
 
-def first_kernel(x_ref, qkv_hbm, rows_ref, proj_hbm, gain_ref, *rest):
-    outs, (bias, mask, attended, mixed, qkv_ref, proj_ref, arrived) = rest[:4], rest[4:]
+def first_kernel(*refs):
+    quarters, (qkv_hbm, rows_ref, proj_hbm, gain_ref, *rest) = refs[:4], refs[4:]
+    outs, (x_ref, bias, mask, attended, mixed, qkv_ref, proj_ref, arrived) = rest[:4], rest[4:]
     block = attended.shape[0]
     heads = block // HD
 
@@ -193,6 +202,7 @@
     for i in range(x_ref.shape[1] // block):
         for copy in copies(i):
             copy.start()
+    lay(quarters, x_ref)
     down = lax.broadcasted_iota(jnp.int32, (TOKENS, TOKENS), 0) // TILE
     across = lax.broadcasted_iota(jnp.int32, (TOKENS, TOKENS), 1) // TILE
     apart = jnp.where(down % 2 != across % 2, rows_ref[0][1:2, 31:32], 0.0)
@@ -228,16 +238,17 @@
             ]
 
 
-def first_attention(x, qkv, rows, proj, gain):
-    chans = x.shape[1]
+def first_attention(quarters, qkv, rows, proj, gain):
+    chans = quarters[0].shape[1]
     vmem = pl.BlockSpec(memory_space=pltpu.VMEM)
     anywhere = pl.BlockSpec(memory_space=pltpu.HBM)
     return pl.pallas_call(
         first_kernel,
-        in_specs=[vmem, anywhere, vmem, anywhere, vmem],
+        in_specs=[vmem] * 4 + [anywhere, vmem, anywhere, vmem],
         out_specs=[vmem] * 4,
         out_shape=[jax.ShapeDtypeStruct((16, 4 * chans), jnp.bfloat16)] * 4,
         scratch_shapes=[
+            pltpu.VMEM((TOKENS, chans), jnp.bfloat16),
             pltpu.VMEM((2, TOKENS, TOKENS), jnp.float32),
             pltpu.VMEM((TOKENS, TOKENS), jnp.float32),
             pltpu.VMEM((2 * LANES, TOKENS), jnp.bfloat16),
@@ -248,10 +259,10 @@
         ],
         compiler_params=pltpu.CompilerParams(vmem_limit_bytes=MOST),
         name="first_attention",
-    )(x, qkv, rows, proj, gain)
-
-
-PIECES = 6
+    )(*quarters, qkv, rows, proj, gain)
+
+
+PIECES = 7
 
 
 def lay(pieces, whole):
@@ -260,6 +271,16 @@
         rows = piece.shape[0]
         whole[at : at + rows, :] = piece[...]
         at += rows
+
+
+def rows_of(pieces, whole):
+    pairs = []
+    at = 0
+    for piece in pieces:
+        rows = piece.shape[0]
+        pairs.append((piece, whole.at[at : at + rows, :]))
+        at += rows
+    return pairs
 
 
 def fetch(pairs, arrived):
@@ -277,14 +298,15 @@
         copy.wait()
 
 
-def merge_kernel(core_ref, *refs):
-    pieces, (own_hbm, other_hbm, out_ref, x, weight, arrived) = (
-        refs[:PIECES],
-        refs[PIECES:],
-    )
-    copies = fetch([(own_hbm, weight.at[:, :LANES]), (other_hbm, weight.at[:, LANES:])], arrived)
-    lay(pieces, x)
-    land(copies)
+def merge_kernel(count, core_ref, *refs):
+    pieces, (own_hbm, other_hbm, out_ref, x, weight, arrived) = refs[:count], refs[count:]
+    land(
+        fetch(
+            [(own_hbm, weight.at[:, :LANES]), (other_hbm, weight.at[:, LANES:])]
+            + rows_of(pieces, x),
+            arrived,
+        )
+    )
     both = jnp.dot(x[...], weight[...], preferred_element_type=jnp.float32).astype(jnp.bfloat16)
     own, other = both[:, :LANES], both[:, LANES:]
     first = core_ref[0] == 0
@@ -297,14 +319,14 @@
     vmem = pl.BlockSpec(memory_space=pltpu.VMEM)
     tokens = GROUP * TILE
     return pl.pallas_call(
-        merge_kernel,
-        in_specs=[smem] + [vmem] * PIECES + [pl.BlockSpec(memory_space=pltpu.HBM)] * 2,
+        functools.partial(merge_kernel, len(pieces)),
+        in_specs=[smem] + [pl.BlockSpec(memory_space=pltpu.HBM)] * (len(pieces) + 2),
         out_specs=vmem,
         out_shape=jax.ShapeDtypeStruct((tokens, 2 * LANES), jnp.bfloat16),
         scratch_shapes=[
             pltpu.VMEM((tokens, pieces[0].shape[1]), jnp.bfloat16),
             pltpu.VMEM((own.shape[0], 2 * LANES), jnp.bfloat16),
-            pltpu.SemaphoreType.DMA((2,)),
+            pltpu.SemaphoreType.DMA((len(pieces) + 2,)),
         ],
         compiler_params=pltpu.CompilerParams(vmem_limit_bytes=MOST - 3 * 1024 * 1024),
         name="merge_patches",
@@ -315,25 +337,32 @@
     parts, refs = refs[:PIECES], refs[PIECES:]
     qkv_refs, rows_refs, proj_refs, gain_ref = refs[0:2], refs[2:4], refs[4:6], refs[6]
     merged_ref, outs = refs[7], refs[8:14]
-    merged, bias, attended, sums, qkv, proj, arrived = refs[14:]
+    merged, bias, attended, sums, qkv, proj, gathered, arrived = refs[14:]
     sides = (slice(0, LANES), slice(LANES, 2 * LANES))
+    pieces_at = [0]
+    for piece in parts[:-1]:
+        pieces_at.append(pieces_at[-1] + piece.shape[0])
     copies = fetch(
-        [(qkv_refs[i], qkv.at[:, :, sides[i]]) for i in range(2)]
+        rows_of(parts, gathered)
+        + [(qkv_refs[i], qkv.at[:, :, sides[i]]) for i in range(2)]
         + [(proj_refs[i], proj.at[sides[i], :]) for i in range(2)],
         arrived,
     )
     wide = 2 * LANES
     half = TILE // 2
     whole = GROUP * wide
+    land(copies[:PIECES])
+    copies = copies[PIECES:]
     for dy, dz, part in ((dy, dz, part) for dy, dz in ORDER for part in range(2)):
         row = pl.multiple_of(at_ref[dy * 2 + dz] * TILE + part * half, half)
         pieces = []
         for fy, fz in MEMBERS:
             index = ORDER.index((fy, fz))
-            source, start = (index, 0) if index < 4 else (2 + index // 2, index % 2)
+            source, start = (index, 0) if index < 6 else (6, index % 2)
             block = ORDER.index(((dy - fy) % 4, dz ^ fz))
             start = start * GROUP * TILE + block * TILE + part * half
-            piece = parts[source][start : start + half, :]
+            start += pieces_at[source]
+            piece = gathered[start : start + half, :]
             pieces.append(piece.astype(jnp.float32))
         mean = sum(jnp.sum(piece, axis=-1, keepdims=True) for piece in pieces) / whole
         pieces = [piece - mean for piece in pieces]
@@ -356,7 +385,7 @@
     for dy, dz in MEMBERS:
         place = at_ref[-dy % 4 * 2 + dz]
         values = sums[pl.ds(pl.multiple_of(place * TILE, TILE), TILE), :]
-        put_part(outs, dy, dz, 0, 0, sums.shape[1], values)
+        put_part(outs, dy, dz, 0, values)
 
 
 def second_attention(at, parts, qkv, rows, proj, gain):
@@ -369,8 +398,7 @@
     return pl.pallas_call(
         second_kernel,
         in_specs=[smem]
-        + [vmem] * PIECES
-        + [anywhere] * 2
+        + [anywhere] * (PIECES + 2)
         + [vmem] * 2
         + [anywhere] * 2
         + [vmem],
@@ -383,7 +411,8 @@
             pltpu.VMEM((tokens, chans), jnp.bfloat16),
             pltpu.VMEM((3, chans, 2 * LANES), jnp.bfloat16),
             pltpu.VMEM((2 * LANES, chans), jnp.bfloat16),
-            pltpu.SemaphoreType.DMA((4,)),
+            pltpu.VMEM((GROUP * tokens, 2 * LANES), jnp.bfloat16),
+            pltpu.SemaphoreType.DMA((PIECES + 4,)),
         ],
         compiler_params=pltpu.CompilerParams(vmem_limit_bytes=MOST - 2 * 1024 * 1024),
         name="second_attention",
@@ -414,7 +443,7 @@
         total = total.astype(jnp.bfloat16)
         for dy, dz in MEMBERS:
             at = ORDER.index((-dy % 4, dz)) * TILE
-            put_part(outs, dy, dz, 0, start, chans, total[at : at + TILE])
+            put_part(outs, dy, dz, start, total[at : at + TILE])
 
 
 def feed_forward(pieces, expand, reduce):
@@ -439,55 +468,36 @@
     )(*pieces, *expand, *reduce)
 
 
-def add_up(parts, count):
-    total = sum(part.astype(jnp.float32) for part in parts).astype(jnp.bfloat16)
-    return [total[i * TILE : (i + 1) * TILE] for i in range(count)]
-
-
-def join_kernel(count, bases, *refs):
-    lows, highs, refs = refs[: count[0]], refs[count[0] : sum(count)], refs[sum(count) :]
-    base, gain_ref, outs = refs[:bases], refs[bases], refs[bases + 1 :]
-    low, high = (sum(part[...].astype(jnp.float32) for part in parts) for parts in (lows, highs))
-    total = norm(jnp.concatenate([low, high], axis=1), gain_ref[...])
-    base = jnp.concatenate([part[...] for part in base], axis=0)
-    total = (base.astype(jnp.float32) + total).astype(jnp.bfloat16)
-    at = 0
-    for out_ref in outs:
-        rows = out_ref.shape[0]
-        out_ref[...] = total[at : at + rows]
-        at += rows
-
-
-def join(lows, highs, base, gain, outs):
+def join_kernel(count, *refs):
+    parts, (base_ref, gain_ref, out_ref) = refs[:count], refs[count:]
+    total = sum(part[:TILE, :].astype(jnp.float32) for part in parts)
+    out_ref[...] = (base_ref[...].astype(jnp.float32) + norm(total, gain_ref[...])).astype(
+        jnp.bfloat16
+    )
+
+
+def join(parts, base, gain):
     vmem = pl.BlockSpec(memory_space=pltpu.VMEM)
-    shape = jax.ShapeDtypeStruct((TILE // outs, gain.shape[1]), jnp.bfloat16)
     return pl.pallas_call(
-        functools.partial(join_kernel, (len(lows), len(highs)), len(base)),
-        in_specs=[vmem] * (len(lows) + len(highs) + len(base) + 1),
-        out_specs=[vmem] * outs,
-        out_shape=[shape] * outs,
+        functools.partial(join_kernel, len(parts)),
+        in_specs=[vmem] * (len(parts) + 2),
+        out_specs=vmem,
+        out_shape=jax.ShapeDtypeStruct(base.shape, jnp.bfloat16),
         compiler_params=pltpu.CompilerParams(vmem_limit_bytes=VMEM),
         name="join_sums",
-    )(*lows, *highs, *base, gain)
+    )(*parts, base, gain)
 
 
 def part_shapes(chans):
-    low = jax.ShapeDtypeStruct((2 * TILE, chans // 2), jnp.bfloat16)
-    high = jax.ShapeDtypeStruct((4 * TILE, chans // 2), jnp.bfloat16)
-    return [low] * 4 + [high] * 2
-
-
-def put_part(outs, dy, dz, start, col, chans, values):
-    rows, wide = values.shape
-    middle = chans // 2
-    if col < middle:
-        at = dz * TILE + start
-        low = min(wide, middle - col)
-        outs[dy][at : at + rows, col : col + low] = values[:, :low]
-    if col + wide > middle:
-        at = dy * TILE + start
-        skip = max(middle - col, 0)
-        outs[4 + dz][at : at + rows, col + skip - middle : col + wide - middle] = values[:, skip:]
+    one = jax.ShapeDtypeStruct((TILE, chans), jnp.bfloat16)
+    two = jax.ShapeDtypeStruct((2 * TILE, chans), jnp.bfloat16)
+    return [one] * 4 + [two] * 2
+
+
+def put_part(outs, dy, dz, col, values):
+    index = ORDER.index((dy, dz))
+    out_ref, start = (outs[index], 0) if index < 4 else (outs[2 + index // 2], index % 2 * TILE)
+    out_ref[start : start + TILE, col : col + values.shape[1]] = values
 
 
 def on_device(
@@ -530,12 +540,12 @@
     corner, below, beside, rows_three = lax.optimization_barrier(
         (corner, below, beside, rows_three)
     )
-    x = jnp.concatenate([corner_of, below, beside, corner], axis=0)
     weights = (merge_weight, qkv_four, proj_four, expand_weight, reduce_weight)
-    x, weights = lax.optimization_barrier((x, weights))
+    quarters = [corner_of, below, beside, corner]
+    quarters, weights = lax.optimization_barrier((quarters, weights))
     merge_weight, qkv_four, proj_four, expand_weight, reduce_weight = weights
     swapped = [other_core(value) for value in weights]
-    quadrants = first_attention(x, qkv_three, rows_three, proj_three, gain_three[None])
+    quadrants = first_attention(quarters, qkv_three, rows_three, proj_three, gain_three[None])
     quadrants, swapped, table_four = lax.optimization_barrier((quadrants, swapped, table_four))
     merge_other, qkv_other, proj_other, expand_other, reduce_other = swapped
 
@@ -550,7 +560,9 @@
     tile = jnp.concatenate(list(halves), axis=0).reshape(TILE, -1)
     rows_four = table_rows(table_four, scale_four)
     rows_other = other_core(rows_four)
-    reduced = merge(core[None].astype(jnp.int32), gather(tile), merge_weight, merge_other)
+    reduced = merge(
+        core[None].astype(jnp.int32), gather(tile, steps=True), merge_weight, merge_other
+    )
 
     dy = jnp.arange(GROUP, dtype=jnp.int32) // 2
     dz = jnp.arange(GROUP, dtype=jnp.int32) % 2
@@ -566,15 +578,11 @@
         (proj_four, proj_other),
         merge_gain[None],
     )
-    after = join(*scatter(parts[:4], parts[4:]), [merged], gain_attend[None], 1)
-
+    after = join(scatter(parts), merged, gain_attend[None])
     parts = feed_forward(
-        gather(*after),
-        (expand_weight, expand_other),
-        (reduce_weight, reduce_other),
-    )
-    (out,) = join(*scatter(parts[:4], parts[4:]), after, gain_feed[None], 1)
-    out = permute(out, unhome)
+        gather(after), (expand_weight, expand_other), (reduce_weight, reduce_other)
+    )
+    out = permute(join(scatter(parts), after, gain_feed[None]), unhome)
     return out.reshape(1, half, half, out.shape[1])
 
 

time: 249 us -> 238 us (0.956)
  waiting for transfers between devices: 111 us -> 107 us
  other arithmetic: 11.7 us -> 8.75 us
    concatenate x4 -> x0, other arithmetic: 4.88 us -> none  [the longest x3 3.05 us: gather(): far = send(jnp.concatenate([value, side], axis=0), 2, 0)]
    ppermute x45 -> x43, waiting for transfers between devices: 111 us -> 107 us  [permute(): return lax.ppermute(value, ('row', 'col'), pairs)]
    slice x4 -> x3, local copies, waits for them, and re-layouts: 0.11 us -> 2.62 us  [the longest x1 1.89 us: on_device(): image[half:, :half]]
    ppermute x45 -> x43, starting transfers between devices: 70 us -> 68.3 us  [permute(): return lax.ppermute(value, ('row', 'col'), pairs)]
  transfers between devices with their start and end apart: 45 -> 43, of which waited for: 27 -> 24; matrix products, arithmetic and copies ran while one was open for 5% -> 5% of each run, Pallas kernels for 7% -> 8%
where the time goes in v1:
time: 238 us; the launch traced here: 236 us
  waiting for transfers between devices  107 us (45%)
  starting transfers between devices  68.3 us (29%)
  Pallas kernels  42.5 us (18%)
  local copies, waits for them, and re-layouts  9.01 us (4%)
  other arithmetic  8.75 us (4%)
    ppermute x43, waiting for transfers between devices, permute(): return lax.ppermute(value, ('row', 'col'), pairs)  107 us
    ppermute x43, starting transfers between devices, permute(): return lax.ppermute(value, ('row', 'col'), pairs)  68.3 us
    pallas_call x1, Pallas kernels, first_attention(): pl.pallas_call(first_kernel, in_specs=[vmem] * 4 + [anywhere, vmem, anywh...  18.2 us
    pallas_call x1, Pallas kernels, second_attention(): pl.pallas_call(second_kernel, in_specs=[smem] + [anywhere] * (PIECES + 2)...  13.3 us
    pallas_call x1, Pallas kernels, feed_forward(): pl.pallas_call(feed_kernel, in_specs=[vmem] * PIECES + [pl.BlockSpec(memo...  5.38 us
    pallas_call x1, Pallas kernels, merge(): pl.pallas_call(functools.partial(merge_kernel, len(pieces)), in_specs=[sm...  4.86 us
  transfers between devices with their start and end apart: 43, of which 24 were waited for; matrix products, arithmetic and copies ran while one was open for 5% of the time, Pallas kernels for 8%

profile of v1, /device:TPU:32, one launch (start us, length us, event | category | flops | bytes accessed | tf_op | source)
XLA Modules:
  0.0 236.0 jit_solution(660162983770906418)
XLA Ops:
  1.9 3.8 %collective-permute-start = (bf16[8,8,1024]{2,1,0:T(8,128)(2,1)}, bf16[8,8,1024]{2,1,0:T(8,128)(2,1)S(1)}, u32[]{:S(2)}, u32[]{:S(2)}) collective-permute-start(bf16[8,8,1024]{2,1,0:T(8,128)(2,1)} %get-tuple-element.91), channel_id=1, source_target_pairs={{0,127},{1,120},{2,121},{3,122},{4,123},{5,124},{6,125},{7,126},{8... | collective-permute-start | bytes 393224 | tf_op jit(solution)/shard_map/ppermute | solution.py:40
  7.4 4.4 %collective-permute-start.2 = (bf16[8,8,1024]{2,1,0:T(8,128)(2,1)}, bf16[8,8,1024]{2,1,0:T(8,128)(2,1)S(1)}, u32[]{:S(2)}, u32[]{:S(2)}) collective-permute-start(bf16[8,8,1024]{2,1,0:T(8,128)(2,1)} %get-tuple-element.89), channel_id=1, source_target_pairs={{0,7},{1,0},{2,1},{3,2},{4,3},{5,4},{6,5},{7,6},{8,15},{9,8},{10,9... | collective-permute-start | bytes 393224 | tf_op jit(solution)/shard_map/ppermute | solution.py:40
  17.9 18.2 %first_attention.1 = (bf16[16,4096]{1,0:T(8,128)(2,1)}, bf16[16,4096]{1,0:T(8,128)(2,1)}, bf16[16,4096]{1,0:T(8,128)(2,1)}, bf16[16,4096]{1,0:T(8,128)(2,1)}) custom-call(bf16[64,1024]{1,0:T(8,128)(2,1)} %get-tuple-element.48.refs_0_, bf16[64,1024]{1,0:T(8,128)(2,1)} %bitcast.43, bf16[64,1024]{1,0:T(8,128)(2,1)} %bitcast.44, bf16[64,1024]{1,0:T(8,128)(2,1)} %bitcast.42, ...), custom_call_target="tpu_custom_call" | custom-call | tf_op jit(solution)/shard_map/first_attention/pallas_call | solution.py:245
  47.4 4.0 %collective-permute-done.11 = bf16[16,4096]{1,0:T(8,128)(2,1)S(1)} collective-permute-done((bf16[16,4096]{1,0:T(8,128)(2,1)}, bf16[16,4096]{1,0:T(8,128)(2,1)S(1)}, u32[]{:S(2)}, u32[]{:S(2)}) %collective-permute-start.11) | collective-permute-done | bytes 131104 | tf_op jit(solution)/shard_map/ppermute | solution.py:40
  55.1 12.7 %collective-permute-done.12.refs_1_ = bf16[64,4096]{1,0:T(8,128)(2,1)S(1)} collective-permute-done((bf16[64,4096]{1,0:T(8,128)(2,1)S(1)}, bf16[64,4096]{1,0:T(8,128)(2,1)S(1)}, u32[]{:S(2)}, u32[]{:S(2)}) %collective-permute-start.12) | collective-permute-done | bytes 524320 | tf_op jit(solution)/shard_map/ppermute | solution.py:40
  75.9 14.4 %collective-permute-done.15.refs_4_ = bf16[32,4096]{1,0:T(8,128)(2,1)} collective-permute-done((bf16[32,4096]{1,0:T(8,128)(2,1)S(1)}, bf16[32,4096]{1,0:T(8,128)(2,1)}, u32[]{:S(2)}, u32[]{:S(2)}) %collective-permute-start.15) | collective-permute-done | bytes 262176 | tf_op jit(solution)/shard_map/ppermute | solution.py:40
  90.4 4.0 %collective-permute-done.18.refs_7_ = bf16[128,4096]{1,0:T(8,128)(2,1)} collective-permute-done((bf16[128,4096]{1,0:T(8,128)(2,1)}, bf16[128,4096]{1,0:T(8,128)(2,1)}, u32[]{:S(2)}, u32[]{:S(2)}) %collective-permute-start.18) | collective-permute-done | bytes 1048608 | tf_op jit(solution)/shard_map/ppermute | solution.py:40
  94.4 4.9 %merge_patches.1.refs_0_ = bf16[512,256]{1,0:T(8,128)(2,1)} custom-call(s32[1]{0:T(128)} %bitcast.core_ref, bf16[64,4096]{1,0:T(8,128)(2,1)} %copy-done.8, bf16[64,4096]{1,0:T(8,128)(2,1)} %copy-done.6, bf16[64,4096]{1,0:T(8,128)(2,1)} %copy-done.7, bf16[64,4096]{1,0:T(8,128)(2,1)} %collective-permute-done.14.refs_3_, ...), custom_call_target="tpu_custom_call" | custom-call | tf_op jit(solution)/shard_map/merge_patches/pallas_call | solution.py:321
  103.2 4.9 %collective-permute-done.19.refs_1_ = bf16[512,256]{1,0:T(8,128)(2,1)S(1)} collective-permute-done((bf16[512,256]{1,0:T(8,128)(2,1)}, bf16[512,256]{1,0:T(8,128)(2,1)S(1)}, u32[]{:S(2)}, u32[]{:S(2)}) %collective-permute-start.19) | collective-permute-done | bytes 262176 | tf_op jit(solution)/shard_map/ppermute | solution.py:40
  115.5 5.7 %collective-permute-done.22.refs_4_ = bf16[512,256]{1,0:T(8,128)(2,1)} collective-permute-done((bf16[512,256]{1,0:T(8,128)(2,1)}, bf16[512,256]{1,0:T(8,128)(2,1)}, u32[]{:S(2)}, u32[]{:S(2)}) %collective-permute-start.22) | collective-permute-done | bytes 262176 | tf_op jit(solution)/shard_map/ppermute | solution.py:40
  121.3 2.9 %collective-permute-done.23.refs_5_ = bf16[512,256]{1,0:T(8,128)(2,1)} collective-permute-done((bf16[512,256]{1,0:T(8,128)(2,1)S(1)}, bf16[512,256]{1,0:T(8,128)(2,1)}, u32[]{:S(2)}, u32[]{:S(2)}) %collective-permute-start.23) | collective-permute-done | bytes 262176 | tf_op jit(solution)/shard_map/ppermute | solution.py:40
  125.0 13.3 %second_attention.1 = (bf16[64,2048]{1,0:T(8,128)(2,1)}, bf16[64,2048]{1,0:T(8,128)(2,1)}, bf16[64,2048]{1,0:T(8,128)(2,1)}, bf16[64,2048]{1,0:T(8,128)(2,1)}, b...) custom-call(s32[16]{0:T(128)} %pad_add_fusion.at_ref, ...), custom_call_target="tpu_custom_call" | custom-call | tf_op jit(solution)/shard_map/second_attention/pallas_call | solution.py:398
  141.4 9.8 %collective-permute-done.26.refs_1_ = bf16[128,2048]{1,0:T(8,128)(2,1)S(1)} collective-permute-done((bf16[128,2048]{1,0:T(8,128)(2,1)}, bf16[128,2048]{1,0:T(8,128)(2,1)S(1)}, u32[]{:S(2)}, u32[]{:S(2)}) %collective-permute-start.26) | collective-permute-done | bytes 524320 | tf_op jit(solution)/shard_map/ppermute | solution.py:40
  158.7 4.3 %collective-permute-done.28.refs_2_ = bf16[64,2048]{1,0:T(8,128)(2,1)S(1)} collective-permute-done((bf16[64,2048]{1,0:T(8,128)(2,1)S(1)}, bf16[64,2048]{1,0:T(8,128)(2,1)S(1)}, u32[]{:S(2)}, u32[]{:S(2)}) %collective-permute-start.28) | collective-permute-done | bytes 262176 | tf_op jit(solution)/shard_map/ppermute | solution.py:40
  163.5 3.5 %collective-permute-start.32 = (bf16[64,2048]{1,0:T(8,128)(2,1)S(1)}, bf16[64,2048]{1,0:T(8,128)(2,1)S(1)}, u32[]{:S(2)}, u32[]{:S(2)}) collective-permute-start(bf16[64,2048]{1,0:T(8,128)(2,1)S(1)} %join_sums.2.refs_0_.refs_5_), channel_id=1, source_target_pairs={{0,48},{1,49},{2,50},{3,51},{4,52},{5,53},{6,54},{7,55},{8,56},{9,... | collective-permute-start | bytes 786440 | tf_op jit(solution)/shard_map/ppermute | solution.py:40
  168.0 4.8 %collective-permute-done.31.refs_1_ = bf16[64,2048]{1,0:T(8,128)(2,1)S(1)} collective-permute-done((bf16[64,2048]{1,0:T(8,128)(2,1)S(1)}, bf16[64,2048]{1,0:T(8,128)(2,1)S(1)}, u32[]{:S(2)}, u32[]{:S(2)}) %collective-permute-start.31) | collective-permute-done | bytes 262176 | tf_op jit(solution)/shard_map/ppermute | solution.py:40
  172.7 3.8 %collective-permute-done.32.refs_2_ = bf16[64,2048]{1,0:T(8,128)(2,1)S(1)} collective-permute-done((bf16[64,2048]{1,0:T(8,128)(2,1)S(1)}, bf16[64,2048]{1,0:T(8,128)(2,1)S(1)}, u32[]{:S(2)}, u32[]{:S(2)}) %collective-permute-start.32) | collective-permute-done | bytes 262176 | tf_op jit(solution)/shard_map/ppermute | solution.py:40
  181.1 4.3 %collective-permute-done.34.refs_4_ = bf16[64,2048]{1,0:T(8,128)(2,1)S(1)} collective-permute-done((bf16[64,2048]{1,0:T(8,128)(2,1)S(1)}, bf16[64,2048]{1,0:T(8,128)(2,1)S(1)}, u32[]{:S(2)}, u32[]{:S(2)}) %collective-permute-start.34) | collective-permute-done | bytes 262176 | tf_op jit(solution)/shard_map/ppermute | solution.py:40
  185.5 3.3 %collective-permute-done.35.refs_5_ = bf16[64,2048]{1,0:T(8,128)(2,1)S(1)} collective-permute-done((bf16[64,2048]{1,0:T(8,128)(2,1)S(1)}, bf16[64,2048]{1,0:T(8,128)(2,1)S(1)}, u32[]{:S(2)}, u32[]{:S(2)}) %collective-permute-start.35) | collective-permute-done | bytes 262176 | tf_op jit(solution)/shard_map/ppermute | solution.py:40
  188.8 5.4 %feed_forward.1 = (bf16[64,2048]{1,0:T(8,128)(2,1)S(1)}, bf16[64,2048]{1,0:T(8,128)(2,1)S(1)}, bf16[64,2048]{1,0:T(8,128)(2,1)S(1)}, bf16[64,2048]{1,0:T(8,128)(...) custom-call(bf16[64,2048]{1,0:T(8,128)(2,1)S(1)} %join_sums.2.refs_0_.refs_5_, ...), custom_call_target="tpu_custom_call" | custom-call | tf_op jit(solution)/shard_map/feed_forward/pallas_call | solution.py:454
  197.0 10.7 %collective-permute-done.37.refs_1_ = bf16[128,2048]{1,0:T(8,128)(2,1)S(1)} collective-permute-done((bf16[128,2048]{1,0:T(8,128)(2,1)S(1)}, bf16[128,2048]{1,0:T(8,128)(2,1)S(1)}, u32[]{:S(2)}, u32[]{:S(2)}) %collective-permute-start.37) | collective-permute-done | bytes 524320 | tf_op jit(solution)/shard_map/ppermute | solution.py:40
  214.3 2.8 %collective-permute-done.39.refs_2_ = bf16[64,2048]{1,0:T(8,128)(2,1)S(1)} collective-permute-done((bf16[64,2048]{1,0:T(8,128)(2,1)S(1)}, bf16[64,2048]{1,0:T(8,128)(2,1)S(1)}, u32[]{:S(2)}, u32[]{:S(2)}) %collective-permute-start.39) | collective-permute-done | bytes 262176 | tf_op jit(solution)/shard_map/ppermute | solution.py:40
  218.2 10.4 %collective-permute-start.42 = (bf16[64,2048]{1,0:T(8,128)(2,1)S(1)}, bf16[64,2048]{1,0:T(8,128)(2,1)S(1)}, u32[]{:S(2)}, u32[]{:S(2)}) collective-permute-start(bf16[64,2048]{1,0:T(8,128)(2,1)S(1)} %join_sums.3), channel_id=1, source_target_pairs={{0,0},{1,65},{2,2},{3,67},{4,4},{5,69},{6,6},{7,71},{8,16},{9,81},... | collective-permute-start | bytes 786440 | tf_op jit(solution)/shard_map/ppermute | solution.py:40
  228.6 6.7 %collective-permute-done.42 = bf16[64,2048]{1,0:T(8,128)(2,1)S(1)} collective-permute-done((bf16[64,2048]{1,0:T(8,128)(2,1)S(1)}, bf16[64,2048]{1,0:T(8,128)(2,1)S(1)}, u32[]{:S(2)}, u32[]{:S(2)}) %collective-permute-start.42) | collective-permute-done | bytes 262176 | tf_op jit(solution)/shard_map/ppermute | solution.py:40
  (149 shorter events, 72.6 us)
Async XLA Ops:
  1.9 14.7 %collective-permute-start = (bf16[8,8,1024]{2,1,0:T(8,128)(2,1)}, bf16[8,8,1024]{2,1,0:T(8,128)(2,1)S(1)}, u32[]{:S(2)}, u32[]{:S(2)}) collective-permute-start(bf16[8,8,1024]{2,1,0:T(8,128)(2,1)} %get-tuple-element.91), channel_id=1, source_target_pairs={{0,127},{1,120},{2,121},{3,122},{4,123},{5,124},{6,125},{7,126},{8... | collective-permute-start | bytes 393224 | tf_op jit(solution)/shard_map/ppermute | solution.py:40
  16.7 19.5 %collective-permute-start.6 = (bf16[2048,512]{1,0:T(8,128)(2,1)S(1)}, bf16[2048,512]{1,0:T(8,128)(2,1)}, u32[]{:S(2)}, u32[]{:S(2)}) collective-permute-start(bf16[2048,512]{1,0:T(8,128)(2,1)S(1)} %copy-done), channel_id=1, source_target_pairs={{0,8},{1,9},{2,10},{3,11},{4,12},{5,13},{6,14},{7,15},{8,0},{9,1},... | collective-permute-start | bytes 6291464 | tf_op jit(solution)/shard_map/ppermute | solution.py:40
  16.8 20.6 %collective-permute-start.7 = (bf16[512,2048]{1,0:T(8,128)(2,1)}, bf16[512,2048]{1,0:T(8,128)(2,1)}, u32[]{:S(2)}, u32[]{:S(2)}) collective-permute-start(bf16[512,2048]{1,0:T(8,128)(2,1)} %refs_9_), channel_id=1, source_target_pairs={{0,8},{1,9},{2,10},{3,11},{4,12},{5,13},{6,14},{7,15},{8,0},{9,1},... | collective-permute-start | bytes 6291464 | tf_op jit(solution)/shard_map/ppermute | solution.py:40
  17.3 18.9 %collective-permute-start.4 = (bf16[3,2048,128]{2,1,0:T(8,128)(2,1)}, bf16[3,2048,128]{2,1,0:T(8,128)(2,1)S(1)}, u32[]{:S(2)}, u32[]{:S(2)}) collective-permute-start(bf16[3,2048,128]{2,1,0:T(8,128)(2,1)} %refs_7_), channel_id=1, source_target_pairs={{0,8},{1,9},{2,10},{3,11},{4,12},{5,13},{6,14},{7,15},{8,0},{9,1},... | collective-permute-start | bytes 4718600 | tf_op jit(solution)/shard_map/ppermute | solution.py:40
  17.3 18.8 %collective-permute-start.3 = (bf16[4096,128]{1,0:T(8,128)(2,1)}, bf16[4096,128]{1,0:T(8,128)(2,1)}, u32[]{:S(2)}, u32[]{:S(2)}) collective-permute-start(bf16[4096,128]{1,0:T(8,128)(2,1)} %refs_8_), channel_id=1, source_target_pairs={{0,8},{1,9},{2,10},{3,11},{4,12},{5,13},{6,14},{7,15},{8,0},{9,1},... | collective-permute-start | bytes 3145736 | tf_op jit(solution)/shard_map/ppermute | solution.py:40
  17.8 18.3 %collective-permute-start.5 = (bf16[128,2048]{1,0:T(8,128)(2,1)}, bf16[128,2048]{1,0:T(8,128)(2,1)}, u32[]{:S(2)}, u32[]{:S(2)}) collective-permute-start(bf16[128,2048]{1,0:T(8,128)(2,1)} %refs_11_), channel_id=1, source_target_pairs={{0,8},{1,9},{2,10},{3,11},{4,12},{5,13},{6,14},{7,15},{8,0},{9,1},... | collective-permute-start | bytes 1572872 | tf_op jit(solution)/shard_map/ppermute | solution.py:40
  51.8 16.0 %collective-permute-start.12 = (bf16[64,4096]{1,0:T(8,128)(2,1)S(1)}, bf16[64,4096]{1,0:T(8,128)(2,1)S(1)}, u32[]{:S(2)}, u32[]{:S(2)}) collective-permute-start(bf16[64,4096]{1,0:T(8,128)(2,1)S(1)} %maximum_bitcast_fusion.1.refs_0_), channel_id=1, source_target_pairs={{0,16},{1,17},{2,18},{3,19},{4,20},{5,21},{6,22},{7,23},{8,24},{9,... | collective-permute-start | bytes 1572872 | tf_op jit(solution)/shard_map/ppermute | solution.py:40
  52.3 15.4 %collective-permute-start.13 = (bf16[64,4096]{1,0:T(8,128)(2,1)S(1)}, bf16[64,4096]{1,0:T(8,128)(2,1)S(1)}, u32[]{:S(2)}, u32[]{:S(2)}) collective-permute-start(bf16[64,4096]{1,0:T(8,128)(2,1)S(1)} %maximum_bitcast_fusion.1.refs_0_), channel_id=1, source_target_pairs={{0,48},{1,49},{2,50},{3,51},{4,52},{5,53},{6,54},{7,55},{8,56},{9,... | collective-permute-start | bytes 1572872 | tf_op jit(solution)/shard_map/ppermute | solution.py:40
  55.1 14.3 %collective-permute-start.14 = (bf16[64,4096]{1,0:T(8,128)(2,1)S(1)}, bf16[64,4096]{1,0:T(8,128)(2,1)}, u32[]{:S(2)}, u32[]{:S(2)}) collective-permute-start(bf16[64,4096]{1,0:T(8,128)(2,1)S(1)} %maximum_bitcast_fusion.1.refs_0_), channel_id=1, source_target_pairs={{0,65},{1,64},{2,67},{3,66},{4,69},{5,68},{6,71},{7,70},{8,73},{9,... | collective-permute-start | bytes 1572872 | tf_op jit(solution)/shard_map/ppermute | solution.py:40
  68.9 25.4 %collective-permute-start.18 = (bf16[128,4096]{1,0:T(8,128)(2,1)}, bf16[128,4096]{1,0:T(8,128)(2,1)}, u32[]{:S(2)}, u32[]{:S(2)}) collective-permute-start(bf16[128,4096]{1,0:T(8,128)(2,1)} %pad_maximum_fusion), channel_id=1, source_target_pairs={{0,65},{1,64},{2,67},{3,66},{4,69},{5,68},{6,71},{7,70},{8,73},{9,... | collective-permute-start | bytes 3145736 | tf_op jit(solution)/shard_map/ppermute | solution.py:40
  69.4 21.0 %collective-permute-start.17 = (bf16[64,4096]{1,0:T(8,128)(2,1)}, bf16[64,4096]{1,0:T(8,128)(2,1)}, u32[]{:S(2)}, u32[]{:S(2)}) collective-permute-start(bf16[64,4096]{1,0:T(8,128)(2,1)} %collective-permute-done.14.refs_3_), channel_id=1, source_target_pairs={{0,32},{1,33},{2,34},{3,35},{4,36},{5,37},{6,38},{7,39},{8,40},{9,... | collective-permute-start | bytes 1572872 | tf_op jit(solution)/shard_map/ppermute | solution.py:40
  71.8 18.4 %collective-permute-start.15 = (bf16[32,4096]{1,0:T(8,128)(2,1)S(1)}, bf16[32,4096]{1,0:T(8,128)(2,1)}, u32[]{:S(2)}, u32[]{:S(2)}) collective-permute-start(bf16[32,4096]{1,0:T(8,128)(2,1)S(1)} %slice.52), channel_id=1, source_target_pairs={{0,16},{1,17},{2,18},{3,19},{4,20},{5,21},{6,22},{7,23},{8,24},{9,... | collective-permute-start | bytes 786440 | tf_op jit(solution)/shard_map/ppermute | solution.py:40
  73.6 16.8 %collective-permute-start.16 = (bf16[32,4096]{1,0:T(8,128)(2,1)}, bf16[32,4096]{1,0:T(8,128)(2,1)}, u32[]{:S(2)}, u32[]{:S(2)}) collective-permute-start(bf16[32,4096]{1,0:T(8,128)(2,1)} %slice.53), channel_id=1, source_target_pairs={{0,48},{1,49},{2,50},{3,51},{4,52},{5,53},{6,54},{7,55},{8,56},{9,... | collective-permute-start | bytes 786440 | tf_op jit(solution)/shard_map/ppermute | solution.py:40
  109.0 15.1 %collective-permute-start.24 = (bf16[1024,256]{1,0:T(8,128)(2,1)}, bf16[1024,256]{1,0:T(8,128)(2,1)S(1)}, u32[]{:S(2)}, u32[]{:S(2)}) collective-permute-start(bf16[1024,256]{1,0:T(8,128)(2,1)} %pad_maximum_fusion.1), channel_id=1, source_target_pairs={{0,65},{1,64},{2,67},{3,66},{4,69},{5,68},{6,71},{7,70},{8,73},{9,... | collective-permute-start | bytes 1572872 | tf_op jit(solution)/shard_map/ppermute | solution.py:40
  110.2 11.1 %collective-permute-start.22 = (bf16[512,256]{1,0:T(8,128)(2,1)}, bf16[512,256]{1,0:T(8,128)(2,1)}, u32[]{:S(2)}, u32[]{:S(2)}) collective-permute-start(bf16[512,256]{1,0:T(8,128)(2,1)} %merge_patches.1.refs_0_), channel_id=1, source_target_pairs={{0,32},{1,33},{2,34},{3,35},{4,36},{5,37},{6,38},{7,39},{8,40},{9,... | collective-permute-start | bytes 786440 | tf_op jit(solution)/shard_map/ppermute | solution.py:40
  112.7 11.4 %collective-permute-start.23 = (bf16[512,256]{1,0:T(8,128)(2,1)S(1)}, bf16[512,256]{1,0:T(8,128)(2,1)}, u32[]{:S(2)}, u32[]{:S(2)}) collective-permute-start(bf16[512,256]{1,0:T(8,128)(2,1)S(1)} %collective-permute-done.21.refs_3_), channel_id=1, source_target_pairs={{0,32},{1,33},{2,34},{3,35},{4,36},{5,37},{6,38},{7,39},{8,40},{9,... | collective-permute-start | bytes 786440 | tf_op jit(solution)/shard_map/ppermute | solution.py:40
  138.2 13.0 %collective-permute-start.26 = (bf16[128,2048]{1,0:T(8,128)(2,1)}, bf16[128,2048]{1,0:T(8,128)(2,1)S(1)}, u32[]{:S(2)}, u32[]{:S(2)}) collective-permute-start(bf16[128,2048]{1,0:T(8,128)(2,1)} %get-tuple-element.71), channel_id=1, source_target_pairs={{0,32},{1,33},{2,34},{3,35},{4,36},{5,37},{6,38},{7,39},{8,40},{9,... | collective-permute-start | bytes 1572872 | tf_op jit(solution)/shard_map/ppermute | solution.py:40
  140.3 12.8 %collective-permute-start.27 = (bf16[128,2048]{1,0:T(8,128)(2,1)}, bf16[128,2048]{1,0:T(8,128)(2,1)S(1)}, u32[]{:S(2)}, u32[]{:S(2)}) collective-permute-start(bf16[128,2048]{1,0:T(8,128)(2,1)} %get-tuple-element.73), channel_id=1, source_target_pairs={{0,65},{1,64},{2,67},{3,66},{4,69},{5,68},{6,71},{7,70},{8,73},{9,... | collective-permute-start | bytes 1572872 | tf_op jit(solution)/shard_map/ppermute | solution.py:40
  163.5 13.0 %collective-permute-start.32 = (bf16[64,2048]{1,0:T(8,128)(2,1)S(1)}, bf16[64,2048]{1,0:T(8,128)(2,1)S(1)}, u32[]{:S(2)}, u32[]{:S(2)}) collective-permute-start(bf16[64,2048]{1,0:T(8,128)(2,1)S(1)} %join_sums.2.refs_0_.refs_5_), channel_id=1, source_target_pairs={{0,48},{1,49},{2,50},{3,51},{4,52},{5,53},{6,54},{7,55},{8,56},{9,... | collective-permute-start | bytes 786440 | tf_op jit(solution)/shard_map/ppermute | solution.py:40
  167.0 11.6 %collective-permute-start.33 = (bf16[64,2048]{1,0:T(8,128)(2,1)S(1)}, bf16[64,2048]{1,0:T(8,128)(2,1)S(1)}, u32[]{:S(2)}, u32[]{:S(2)}) collective-permute-start(bf16[64,2048]{1,0:T(8,128)(2,1)S(1)} %join_sums.2.refs_0_.refs_5_), channel_id=1, source_target_pairs={{0,65},{1,64},{2,67},{3,66},{4,69},{5,68},{6,71},{7,70},{8,73},{9,... | collective-permute-start | bytes 786440 | tf_op jit(solution)/shard_map/ppermute | solution.py:40
  176.6 12.2 %collective-permute-start.36 = (bf16[128,2048]{1,0:T(8,128)(2,1)S(1)}, bf16[128,2048]{1,0:T(8,128)(2,1)S(1)}, u32[]{:S(2)}, u32[]{:S(2)}) collective-permute-start(bf16[128,2048]{1,0:T(8,128)(2,1)S(1)} %pad_maximum_fusion.2), channel_id=1, source_target_pairs={{0,65},{1,64},{2,67},{3,66},{4,69},{5,68},{6,71},{7,70},{8,73},{9,... | collective-permute-start | bytes 1572872 | tf_op jit(solution)/shard_map/ppermute | solution.py:40
  194.2 13.6 %collective-permute-start.37 = (bf16[128,2048]{1,0:T(8,128)(2,1)S(1)}, bf16[128,2048]{1,0:T(8,128)(2,1)S(1)}, u32[]{:S(2)}, u32[]{:S(2)}) collective-permute-start(bf16[128,2048]{1,0:T(8,128)(2,1)S(1)} %get-tuple-element.80), channel_id=1, source_target_pairs={{0,32},{1,33},{2,34},{3,35},{4,36},{5,37},{6,38},{7,39},{8,40},{9,... | collective-permute-start | bytes 1572872 | tf_op jit(solution)/shard_map/ppermute | solution.py:40
  196.0 13.3 %collective-permute-start.38 = (bf16[128,2048]{1,0:T(8,128)(2,1)S(1)}, bf16[128,2048]{1,0:T(8,128)(2,1)S(1)}, u32[]{:S(2)}, u32[]{:S(2)}) collective-permute-start(bf16[128,2048]{1,0:T(8,128)(2,1)S(1)} %get-tuple-element.82), channel_id=1, source_target_pairs={{0,65},{1,64},{2,67},{3,66},{4,69},{5,68},{6,71},{7,70},{8,73},{9,... | collective-permute-start | bytes 1572872 | tf_op jit(solution)/shard_map/ppermute | solution.py:40
  218.2 17.1 %collective-permute-start.42 = (bf16[64,2048]{1,0:T(8,128)(2,1)S(1)}, bf16[64,2048]{1,0:T(8,128)(2,1)S(1)}, u32[]{:S(2)}, u32[]{:S(2)}) collective-permute-start(bf16[64,2048]{1,0:T(8,128)(2,1)S(1)} %join_sums.3), channel_id=1, source_target_pairs={{0,0},{1,65},{2,2},{3,67},{4,4},{5,69},{6,6},{7,71},{8,16},{9,81},... | collective-permute-start | bytes 786440 | tf_op jit(solution)/shard_map/ppermute | solution.py:40
  (40 other events, 452.6 us)

commit v2 on v1

--- a/solution.py
+++ b/solution.py
@@ -21,7 +21,7 @@
 ROWS = 16
 COLS = 8
 VMEM = 24 * 1024 * 1024
-MOST = 60 * 1024 * 1024
+MOST = 61 * 1024 * 1024
 LOG2E = math.log2(math.e)
 
 
@@ -64,8 +64,8 @@
 
 
 def gather(value, steps=False):
+    before, after = send(value, 1, 0), send(value, 3, 0)
     side = send(value, 0, 1)
-    before, after = send(value, 1, 0), send(value, 3, 0)
     if steps:
         half = value.shape[0] // 2
         far = [send(before[:half], 1, 0), send(after[half:], 3, 0)]
@@ -298,8 +298,9 @@
         copy.wait()
 
 
-def merge_kernel(count, core_ref, *refs):
-    pieces, (own_hbm, other_hbm, out_ref, x, weight, arrived) = refs[:count], refs[count:]
+def merge_kernel(count, ahead, core_ref, *refs):
+    pieces, refs = refs[:count], refs[count:]
+    own_hbm, other_hbm, *done, out_ref, x, weight, arrived = refs
     land(
         fetch(
             [(own_hbm, weight.at[:, :LANES]), (other_hbm, weight.at[:, LANES:])]
@@ -310,19 +311,24 @@
     both = jnp.dot(x[...], weight[...], preferred_element_type=jnp.float32).astype(jnp.bfloat16)
     own, other = both[:, :LANES], both[:, LANES:]
     first = core_ref[0] == 0
-    out_ref[:, :LANES] = jnp.where(first, own, other)
-    out_ref[:, LANES:] = jnp.where(first, other, own)
-
-
-def merge(core, pieces, own, other):
+    if ahead:
+        out_ref[:ahead, :] = done[0][...]
+    out_ref[ahead:, :LANES] = jnp.where(first, own, other)
+    out_ref[ahead:, LANES:] = jnp.where(first, other, own)
+
+
+def merge(core, pieces, own, other, done=()):
     smem = pl.BlockSpec(memory_space=pltpu.SMEM)
     vmem = pl.BlockSpec(memory_space=pltpu.VMEM)
-    tokens = GROUP * TILE
+    tokens = sum(piece.shape[0] for piece in pieces)
+    ahead = sum(part.shape[0] for part in done)
     return pl.pallas_call(
-        functools.partial(merge_kernel, len(pieces)),
-        in_specs=[smem] + [pl.BlockSpec(memory_space=pltpu.HBM)] * (len(pieces) + 2),
+        functools.partial(merge_kernel, len(pieces), ahead),
+        in_specs=[smem]
+        + [pl.BlockSpec(memory_space=pltpu.HBM)] * (len(pieces) + 2)
+        + [vmem] * len(done),
         out_specs=vmem,
-        out_shape=jax.ShapeDtypeStruct((tokens, 2 * LANES), jnp.bfloat16),
+        out_shape=jax.ShapeDtypeStruct((ahead + tokens, 2 * LANES), jnp.bfloat16),
         scratch_shapes=[
             pltpu.VMEM((tokens, pieces[0].shape[1]), jnp.bfloat16),
             pltpu.VMEM((own.shape[0], 2 * LANES), jnp.bfloat16),
@@ -330,7 +336,7 @@
         ],
         compiler_params=pltpu.CompilerParams(vmem_limit_bytes=MOST - 3 * 1024 * 1024),
         name="merge_patches",
-    )(core, *pieces, own, other)
+    )(core, *pieces, own, other, *done)
 
 
 def second_kernel(at_ref, *refs):
@@ -414,14 +420,14 @@
             pltpu.VMEM((GROUP * tokens, 2 * LANES), jnp.bfloat16),
             pltpu.SemaphoreType.DMA((PIECES + 4,)),
         ],
-        compiler_params=pltpu.CompilerParams(vmem_limit_bytes=MOST - 2 * 1024 * 1024),
+        compiler_params=pltpu.CompilerParams(vmem_limit_bytes=MOST - 3 * 1024 * 1024),
         name="second_attention",
     )(at, *parts, *qkv, *rows, *proj, gain)
 
 
-def feed_kernel(*refs):
-    pieces, refs = refs[:PIECES], refs[PIECES:]
-    outs, (x, hidden, expand, reduce, arrived) = refs[4:10], refs[10:]
+def feed_kernel(count, takes, *refs):
+    pieces, refs = refs[:count], refs[count:]
+    outs, (x, hidden, expand, reduce, arrived) = refs[4 : 4 + len(takes)], refs[4 + len(takes) :]
     units = expand.shape[2]
     copies = fetch(
         [(refs[side], expand.at[side]) for side in range(2)]
@@ -431,31 +437,32 @@
     lay(pieces, x)
     for side in range(2):
         land(copies[side : side + 1])
-        lifted = jnp.dot(x[...], expand[side][...], preferred_element_type=jnp.float32)
+        lifted = jnp.dot(x[...], expand[side], preferred_element_type=jnp.float32)
         values = 0.5 * lifted * (1.0 + lax.erf(lifted * math.sqrt(0.5)))
         hidden[:, side * units : (side + 1) * units] = values.astype(jnp.bfloat16)
     block = 4 * LANES
     chans = reduce.shape[1]
     land(copies[2:])
-    for start in range(0, chans, block):
-        cols = slice(start, start + block)
+    for col in range(0, chans, block):
+        cols = slice(col, col + block)
         total = jnp.dot(hidden[...], reduce[:, cols], preferred_element_type=jnp.float32)
         total = total.astype(jnp.bfloat16)
-        for dy, dz in MEMBERS:
-            at = ORDER.index((-dy % 4, dz)) * TILE
-            put_part(outs, dy, dz, start, total[at : at + TILE])
-
-
-def feed_forward(pieces, expand, reduce):
+        for out_ref, starts in zip(outs, takes):
+            for i, start in enumerate(starts):
+                out_ref[i * TILE : (i + 1) * TILE, cols] = total[start : start + TILE]
+
+
+def feed_half(pieces, expand, reduce, takes):
     chans, units = expand[0].shape
-    tokens = GROUP * TILE
+    tokens = sum(piece.shape[0] for piece in pieces)
     vmem = pl.BlockSpec(memory_space=pltpu.VMEM)
-    shapes = part_shapes(chans)
     return pl.pallas_call(
-        feed_kernel,
-        in_specs=[vmem] * PIECES + [pl.BlockSpec(memory_space=pltpu.HBM)] * 4,
-        out_specs=[vmem] * len(shapes),
-        out_shape=shapes,
+        functools.partial(feed_kernel, len(pieces), takes),
+        in_specs=[vmem] * len(pieces) + [pl.BlockSpec(memory_space=pltpu.HBM)] * 4,
+        out_specs=[vmem] * len(takes),
+        out_shape=[
+            jax.ShapeDtypeStruct((TILE * len(starts), chans), jnp.bfloat16) for starts in takes
+        ],
         scratch_shapes=[
             pltpu.VMEM((tokens, chans), jnp.bfloat16),
             pltpu.VMEM((tokens, 2 * units), jnp.bfloat16),
@@ -466,6 +473,20 @@
         compiler_params=pltpu.CompilerParams(vmem_limit_bytes=VMEM),
         name="feed_forward",
     )(*pieces, *expand, *reduce)
+
+
+def feed_forward(pieces, expand, reduce):
+    rows = {member: ORDER.index(member) * TILE for member in ORDER}
+
+    def takes(group, base):
+        return tuple(tuple(rows[-dy % 4, dz] - base for dy, dz in members) for members in group)
+
+    near = takes((((0, 0),), ((1, 0),), ((3, 0),), ((0, 1),)), 0)
+    far = takes((((2, 0), (2, 1)), ((1, 1), (3, 1))), 4 * TILE)
+    return [
+        *feed_half(pieces[:4], expand, reduce, near),
+        *feed_half(pieces[4:], expand, reduce, far),
+    ]
 
 
 def join_kernel(count, *refs):
@@ -560,9 +581,10 @@
     tile = jnp.concatenate(list(halves), axis=0).reshape(TILE, -1)
     rows_four = table_rows(table_four, scale_four)
     rows_other = other_core(rows_four)
-    reduced = merge(
-        core[None].astype(jnp.int32), gather(tile, steps=True), merge_weight, merge_other
-    )
+    pieces = gather(tile, steps=True)
+    side = core[None].astype(jnp.int32)
+    reduced = merge(side, pieces[:4], merge_weight, merge_other)
+    reduced = merge(side, pieces[4:], merge_weight, merge_other, (reduced,))
 
     dy = jnp.arange(GROUP, dtype=jnp.int32) // 2
     dz = jnp.arange(GROUP, dtype=jnp.int32) % 2

time: 238 us -> 235 us (0.987)
  starting transfers between devices: 68.3 us -> 54.7 us
  waiting for transfers between devices: 107 us -> 115 us
  Pallas kernels: 42.5 us -> 47.9 us
    ppermute x43, starting transfers between devices: 68.3 us -> 54.7 us  [permute(): return lax.ppermute(value, ('row', 'col'), pairs)]
    ppermute x43, waiting for transfers between devices: 107 us -> 115 us  [permute(): return lax.ppermute(value, ('row', 'col'), pairs)]
    pallas_call x2 -> x4, Pallas kernels: 10.2 us -> 15.6 us  [the longest x2 8.1 us: merge(): pl.pallas_call(functools.partial(merge_kernel, len(pieces), ahead), in_sp...]
  transfers between devices with their start and end apart: 43 -> 43, of which waited for: 24 -> 26; matrix products, arithmetic and copies ran while one was open for 5% -> 6% of each run, Pallas kernels for 8% -> 11%
where the time goes in v2:
time: 235 us
  waiting for transfers between devices  115 us (49%)
  starting transfers between devices  54.7 us (23%)
  Pallas kernels  47.9 us (20%)
  other arithmetic  8.61 us (4%)
  local copies, waits for them, and re-layouts  8.56 us (4%)
    ppermute x43, waiting for transfers between devices, permute(): return lax.ppermute(value, ('row', 'col'), pairs)  115 us
    ppermute x43, starting transfers between devices, permute(): return lax.ppermute(value, ('row', 'col'), pairs)  54.7 us
    pallas_call x1, Pallas kernels, first_attention(): pl.pallas_call(first_kernel, in_specs=[vmem] * 4 + [anywhere, vmem, anywh...  18.2 us
    pallas_call x1, Pallas kernels, second_attention(): pl.pallas_call(second_kernel, in_specs=[smem] + [anywhere] * (PIECES + 2)...  13.2 us
    pallas_call x2, Pallas kernels, merge(): pl.pallas_call(functools.partial(merge_kernel, len(pieces), ahead), in_sp...  8.1 us
    pallas_call x2, Pallas kernels, feed_half(): pl.pallas_call(functools.partial(feed_kernel, len(pieces), takes), in_spe...  7.51 us
  transfers between devices with their start and end apart: 43, of which 26 were waited for; matrix products, arithmetic and copies ran while one was open for 6% of the time, Pallas kernels for 11%

profile of v2, /device:TPU:32, one launch (start us, length us, event | category | flops | bytes accessed | tf_op | source)
XLA Modules:
  0.0 235.1 jit_solution(7508082522629605544)
XLA Ops:
  1.9 5.0 %collective-permute-start.1 = (bf16[8,8,1024]{2,1,0:T(8,128)(2,1)}, bf16[8,8,1024]{2,1,0:T(8,128)(2,1)S(1)}, u32[]{:S(2)}, u32[]{:S(2)}) collective-permute-start(bf16[8,8,1024]{2,1,0:T(8,128)(2,1)} %get-tuple-element.90), channel_id=1, source_target_pairs={{0,120},{1,121},{2,122},{3,123},{4,124},{5,125},{6,126},{7,127},{8... | collective-permute-start | bytes 393224 | tf_op jit(solution)/shard_map/ppermute | solution.py:40
  6.9 3.3 %collective-permute-start = (bf16[8,8,1024]{2,1,0:T(8,128)(2,1)}, bf16[8,8,1024]{2,1,0:T(8,128)(2,1)S(1)}, u32[]{:S(2)}, u32[]{:S(2)}) collective-permute-start(bf16[8,8,1024]{2,1,0:T(8,128)(2,1)} %get-tuple-element.91), channel_id=1, source_target_pairs={{0,127},{1,120},{2,121},{3,122},{4,123},{5,124},{6,125},{7,126},{8... | collective-permute-start | bytes 393224 | tf_op jit(solution)/shard_map/ppermute | solution.py:40
  17.4 18.2 %first_attention.1 = (bf16[16,4096]{1,0:T(8,128)(2,1)}, bf16[16,4096]{1,0:T(8,128)(2,1)}, bf16[16,4096]{1,0:T(8,128)(2,1)}, bf16[16,4096]{1,0:T(8,128)(2,1)}) custom-call(bf16[64,1024]{1,0:T(8,128)(2,1)} %get-tuple-element.48.refs_0_, bf16[64,1024]{1,0:T(8,128)(2,1)} %bitcast.43, bf16[64,1024]{1,0:T(8,128)(2,1)} %bitcast.42, bf16[64,1024]{1,0:T(8,128)(2,1)} %bitcast.44, ...), custom_call_target="tpu_custom_call" | custom-call | tf_op jit(solution)/shard_map/first_attention/pallas_call | solution.py:245
  48.5 4.9 %collective-permute-start.14 = (bf16[64,4096]{1,0:T(8,128)(2,1)S(1)}, bf16[64,4096]{1,0:T(8,128)(2,1)S(1)}, u32[]{:S(2)}, u32[]{:S(2)}) collective-permute-start(bf16[64,4096]{1,0:T(8,128)(2,1)S(1)} %maximum_bitcast_fusion.1.refs_0_), channel_id=1, source_target_pairs={{0,48},{1,49},{2,50},{3,51},{4,52},{5,53},{6,54},{7,55},{8,56},{9,... | collective-permute-start | bytes 1572872 | tf_op jit(solution)/shard_map/ppermute | solution.py:40
  53.4 12.3 %collective-permute-done.14.refs_2_ = bf16[64,4096]{1,0:T(8,128)(2,1)S(1)} collective-permute-done((bf16[64,4096]{1,0:T(8,128)(2,1)S(1)}, bf16[64,4096]{1,0:T(8,128)(2,1)S(1)}, u32[]{:S(2)}, u32[]{:S(2)}) %collective-permute-start.14) | collective-permute-done | bytes 524320 | tf_op jit(solution)/shard_map/ppermute | solution.py:40
  65.7 3.5 %collective-permute-done.12.refs_1_ = bf16[64,4096]{1,0:T(8,128)(2,1)S(1)} collective-permute-done((bf16[64,4096]{1,0:T(8,128)(2,1)S(1)}, bf16[64,4096]{1,0:T(8,128)(2,1)S(1)}, u32[]{:S(2)}, u32[]{:S(2)}) %collective-permute-start.12) | collective-permute-done | bytes 524320 | tf_op jit(solution)/shard_map/ppermute | solution.py:40
  73.8 3.6 %merge_patches.2.refs_6_ = bf16[256,256]{1,0:T(8,128)(2,1)} custom-call(s32[1]{0:T(128)} %bitcast.core_ref, bf16[64,4096]{1,0:T(8,128)(2,1)} %copy-done.8, bf16[64,4096]{1,0:T(8,128)(2,1)} %copy-done.7, bf16[64,4096]{1,0:T(8,128)(2,1)} %copy-done.6, bf16[64,4096]{1,0:T(8,128)(2,1)} %collective-permute-done.16.refs_3_, bf16[4096,128]{1,0:T(8,128)(2,1)} %refs_4_.3, ...), custom_call_target="tpu_custom_call" | custom-call | tf_op jit(solution)/shard_map/merge_patches/pallas_call | solution.py:325
  77.4 11.8 %collective-permute-done.15.refs_1_ = bf16[32,4096]{1,0:T(8,128)(2,1)S(1)} collective-permute-done((bf16[32,4096]{1,0:T(8,128)(2,1)}, bf16[32,4096]{1,0:T(8,128)(2,1)S(1)}, u32[]{:S(2)}, u32[]{:S(2)}) %collective-permute-start.15) | collective-permute-done | bytes 262176 | tf_op jit(solution)/shard_map/ppermute | solution.py:40
  91.5 4.1 %collective-permute-done.18.refs_3_ = bf16[128,4096]{1,0:T(8,128)(2,1)} collective-permute-done((bf16[128,4096]{1,0:T(8,128)(2,1)}, bf16[128,4096]{1,0:T(8,128)(2,1)}, u32[]{:S(2)}, u32[]{:S(2)}) %collective-permute-start.18) | collective-permute-done | bytes 1048608 | tf_op jit(solution)/shard_map/ppermute | solution.py:40
  95.6 4.5 %merge_patches.3.refs_0_ = bf16[512,256]{1,0:T(8,128)(2,1)} custom-call(s32[1]{0:T(128)} %bitcast.core_ref, bf16[32,4096]{1,0:T(8,128)(2,1)} %collective-permute-done.13.refs_0_, bf16[32,4096]{1,0:T(8,128)(2,1)} %copy-done.14, bf16[64,4096]{1,0:T(8,128)(2,1)} %collective-permute-done.17.refs_2_, bf16[128,4096]{1,0:T(8,128)(2,1)} %collective-permute-done.18.refs_3_, ...), custom_call_target="tpu_custom_call" | custom-call | tf_op jit(solution)/shard_map/merge_patches/pallas_call | solution.py:325
  102.9 4.7 %collective-permute-done.20.refs_2_ = bf16[512,256]{1,0:T(8,128)(2,1)S(1)} collective-permute-done((bf16[512,256]{1,0:T(8,128)(2,1)}, bf16[512,256]{1,0:T(8,128)(2,1)S(1)}, u32[]{:S(2)}, u32[]{:S(2)}) %collective-permute-start.20) | collective-permute-done | bytes 262176 | tf_op jit(solution)/shard_map/ppermute | solution.py:40
  116.7 5.7 %collective-permute-done.22.refs_4_ = bf16[512,256]{1,0:T(8,128)(2,1)} collective-permute-done((bf16[512,256]{1,0:T(8,128)(2,1)}, bf16[512,256]{1,0:T(8,128)(2,1)}, u32[]{:S(2)}, u32[]{:S(2)}) %collective-permute-start.22) | collective-permute-done | bytes 262176 | tf_op jit(solution)/shard_map/ppermute | solution.py:40
  126.0 13.2 %second_attention.1 = (bf16[64,2048]{1,0:T(8,128)(2,1)}, bf16[64,2048]{1,0:T(8,128)(2,1)}, bf16[64,2048]{1,0:T(8,128)(2,1)}, bf16[64,2048]{1,0:T(8,128)(2,1)}, b...) custom-call(s32[16]{0:T(128)} %pad_add_fusion.at_ref, ...), custom_call_target="tpu_custom_call" | custom-call | tf_op jit(solution)/shard_map/second_attention/pallas_call | solution.py:404
  141.0 11.2 %collective-permute-done.26.refs_1_ = bf16[128,2048]{1,0:T(8,128)(2,1)S(1)} collective-permute-done((bf16[128,2048]{1,0:T(8,128)(2,1)}, bf16[128,2048]{1,0:T(8,128)(2,1)S(1)}, u32[]{:S(2)}, u32[]{:S(2)}) %collective-permute-start.26) | collective-permute-done | bytes 524320 | tf_op jit(solution)/shard_map/ppermute | solution.py:40
  168.5 6.1 %collective-permute-done.32.refs_2_ = bf16[64,2048]{1,0:T(8,128)(2,1)S(1)} collective-permute-done((bf16[64,2048]{1,0:T(8,128)(2,1)S(1)}, bf16[64,2048]{1,0:T(8,128)(2,1)S(1)}, u32[]{:S(2)}, u32[]{:S(2)}) %collective-permute-start.32) | collective-permute-done | bytes 262176 | tf_op jit(solution)/shard_map/ppermute | solution.py:40
  174.6 4.2 %collective-permute-done.31.refs_1_ = bf16[64,2048]{1,0:T(8,128)(2,1)S(1)} collective-permute-done((bf16[64,2048]{1,0:T(8,128)(2,1)S(1)}, bf16[64,2048]{1,0:T(8,128)(2,1)S(1)}, u32[]{:S(2)}, u32[]{:S(2)}) %collective-permute-start.31) | collective-permute-done | bytes 262176 | tf_op jit(solution)/shard_map/ppermute | solution.py:40
  179.9 3.5 %collective-permute-start.35 = (bf16[64,2048]{1,0:T(8,128)(2,1)S(1)}, bf16[64,2048]{1,0:T(8,128)(2,1)S(1)}, u32[]{:S(2)}, u32[]{:S(2)}) collective-permute-start(bf16[64,2048]{1,0:T(8,128)(2,1)S(1)} %collective-permute-done.33.refs_3_), channel_id=1, source_target_pairs={{0,32},{1,33},{2,34},{3,35},{4,36},{5,37},{6,38},{7,39},{8,40},{9,... | collective-permute-start | bytes 786440 | tf_op jit(solution)/shard_map/ppermute | solution.py:40
  183.4 6.3 %collective-permute-done.34.refs_0_ = bf16[64,2048]{1,0:T(8,128)(2,1)S(1)} collective-permute-done((bf16[64,2048]{1,0:T(8,128)(2,1)S(1)}, bf16[64,2048]{1,0:T(8,128)(2,1)S(1)}, u32[]{:S(2)}, u32[]{:S(2)}) %collective-permute-start.34) | collective-permute-done | bytes 262176 | tf_op jit(solution)/shard_map/ppermute | solution.py:40
  189.7 5.6 %collective-permute-done.35.refs_1_ = bf16[64,2048]{1,0:T(8,128)(2,1)S(1)} collective-permute-done((bf16[64,2048]{1,0:T(8,128)(2,1)S(1)}, bf16[64,2048]{1,0:T(8,128)(2,1)S(1)}, u32[]{:S(2)}, u32[]{:S(2)}) %collective-permute-start.35) | collective-permute-done | bytes 262176 | tf_op jit(solution)/shard_map/ppermute | solution.py:40
  195.3 3.8 %feed_forward.3 = (bf16[128,2048]{1,0:T(8,128)(2,1)S(1)}, bf16[128,2048]{1,0:T(8,128)(2,1)S(1)}) custom-call(bf16[64,2048]{1,0:T(8,128)(2,1)S(1)} %collective-permute-done.34.refs_0_, bf16[64,2048]{1,0:T(8,128)(2,1)S(1)} %collective-permute-done.35.refs_1_, bf16[128,2048]{1,0:T(8,128)(2,1)S(1)} %collective-permute-done.36.refs_2_, ...), custom_call_target="tpu_custom_call" | custom-call | tf_op jit(solution)/shard_map/feed_forward/pallas_call | solution.py:459
  200.1 3.8 %feed_forward.2 = (bf16[64,2048]{1,0:T(8,128)(2,1)S(1)}, bf16[64,2048]{1,0:T(8,128)(2,1)S(1)}, bf16[64,2048]{1,0:T(8,128)(2,1)S(1)}, bf16[64,2048]{1,0:T(8,128)(2,1)S(1)}) custom-call(bf16[64,2048]{1,0:T(8,128)(2,1)S(1)} %join_sums.2.refs_0_.refs_5_, bf16[64,2048]{1,0:T(8,128)(2,1)S(1)} %collective-permute-done.31.refs_1_, ...), custom_call_target="tpu_custom_call" | custom-call | tf_op jit(solution)/shard_map/feed_forward/pallas_call | solution.py:459
  203.9 5.9 %collective-permute-done.37.refs_1_ = bf16[128,2048]{1,0:T(8,128)(2,1)S(1)} collective-permute-done((bf16[128,2048]{1,0:T(8,128)(2,1)S(1)}, bf16[128,2048]{1,0:T(8,128)(2,1)S(1)}, u32[]{:S(2)}, u32[]{:S(2)}) %collective-permute-start.37) | collective-permute-done | bytes 524320 | tf_op jit(solution)/shard_map/ppermute | solution.py:40
  219.2 8.2 %collective-permute-start.42 = (bf16[64,2048]{1,0:T(8,128)(2,1)S(1)}, bf16[64,2048]{1,0:T(8,128)(2,1)S(1)}, u32[]{:S(2)}, u32[]{:S(2)}) collective-permute-start(bf16[64,2048]{1,0:T(8,128)(2,1)S(1)} %join_sums.3), channel_id=1, source_target_pairs={{0,0},{1,65},{2,2},{3,67},{4,4},{5,69},{6,6},{7,71},{8,16},{9,81},... | collective-permute-start | bytes 786440 | tf_op jit(solution)/shard_map/ppermute | solution.py:40
  227.4 7.0 %collective-permute-done.42 = bf16[64,2048]{1,0:T(8,128)(2,1)S(1)} collective-permute-done((bf16[64,2048]{1,0:T(8,128)(2,1)S(1)}, bf16[64,2048]{1,0:T(8,128)(2,1)S(1)}, u32[]{:S(2)}, u32[]{:S(2)}) %collective-permute-start.42) | collective-permute-done | bytes 262176 | tf_op jit(solution)/shard_map/ppermute | solution.py:40
  (153 shorter events, 74.2 us)
Async XLA Ops:
  1.9 13.1 %collective-permute-start.2 = (bf16[8,8,1024]{2,1,0:T(8,128)(2,1)}, bf16[8,8,1024]{2,1,0:T(8,128)(2,1)S(1)}, u32[]{:S(2)}, u32[]{:S(2)}) collective-permute-start(bf16[8,8,1024]{2,1,0:T(8,128)(2,1)} %get-tuple-element.89), channel_id=1, source_target_pairs={{0,7},{1,0},{2,1},{3,2},{4,3},{5,4},{6,5},{7,6},{8,15},{9,8},{10,9... | collective-permute-start | bytes 393224 | tf_op jit(solution)/shard_map/ppermute | solution.py:40
  1.9 13.0 %collective-permute-start.1 = (bf16[8,8,1024]{2,1,0:T(8,128)(2,1)}, bf16[8,8,1024]{2,1,0:T(8,128)(2,1)S(1)}, u32[]{:S(2)}, u32[]{:S(2)}) collective-permute-start(bf16[8,8,1024]{2,1,0:T(8,128)(2,1)} %get-tuple-element.90), channel_id=1, source_target_pairs={{0,120},{1,121},{2,122},{3,123},{4,124},{5,125},{6,126},{7,127},{8... | collective-permute-start | bytes 393224 | tf_op jit(solution)/shard_map/ppermute | solution.py:40
  15.0 20.6 %collective-permute-start.6 = (bf16[2048,512]{1,0:T(8,128)(2,1)S(1)}, bf16[2048,512]{1,0:T(8,128)(2,1)}, u32[]{:S(2)}, u32[]{:S(2)}) collective-permute-start(bf16[2048,512]{1,0:T(8,128)(2,1)S(1)} %copy-done), channel_id=1, source_target_pairs={{0,8},{1,9},{2,10},{3,11},{4,12},{5,13},{6,14},{7,15},{8,0},{9,1},... | collective-permute-start | bytes 6291464 | tf_op jit(solution)/shard_map/ppermute | solution.py:40
  16.3 19.3 %collective-permute-start.7 = (bf16[512,2048]{1,0:T(8,128)(2,1)}, bf16[512,2048]{1,0:T(8,128)(2,1)}, u32[]{:S(2)}, u32[]{:S(2)}) collective-permute-start(bf16[512,2048]{1,0:T(8,128)(2,1)} %refs_5_), channel_id=1, source_target_pairs={{0,8},{1,9},{2,10},{3,11},{4,12},{5,13},{6,14},{7,15},{8,0},{9,1},... | collective-permute-start | bytes 6291464 | tf_op jit(solution)/shard_map/ppermute | solution.py:40
  16.4 19.2 %collective-permute-start.4 = (bf16[3,2048,128]{2,1,0:T(8,128)(2,1)}, bf16[3,2048,128]{2,1,0:T(8,128)(2,1)}, u32[]{:S(2)}, u32[]{:S(2)}) collective-permute-start(bf16[3,2048,128]{2,1,0:T(8,128)(2,1)} %refs_7_), channel_id=1, source_target_pairs={{0,8},{1,9},{2,10},{3,11},{4,12},{5,13},{6,14},{7,15},{8,0},{9,1},... | collective-permute-start | bytes 4718600 | tf_op jit(solution)/shard_map/ppermute | solution.py:40
  16.8 18.8 %collective-permute-start.3 = (bf16[4096,128]{1,0:T(8,128)(2,1)}, bf16[4096,128]{1,0:T(8,128)(2,1)}, u32[]{:S(2)}, u32[]{:S(2)}) collective-permute-start(bf16[4096,128]{1,0:T(8,128)(2,1)} %refs_4_.3), channel_id=1, source_target_pairs={{0,8},{1,9},{2,10},{3,11},{4,12},{5,13},{6,14},{7,15},{8,0},{9,1},... | collective-permute-start | bytes 3145736 | tf_op jit(solution)/shard_map/ppermute | solution.py:40
  16.9 18.7 %collective-permute-start.5 = (bf16[128,2048]{1,0:T(8,128)(2,1)}, bf16[128,2048]{1,0:T(8,128)(2,1)S(1)}, u32[]{:S(2)}, u32[]{:S(2)}) collective-permute-start(bf16[128,2048]{1,0:T(8,128)(2,1)} %refs_11_), channel_id=1, source_target_pairs={{0,8},{1,9},{2,10},{3,11},{4,12},{5,13},{6,14},{7,15},{8,0},{9,1},... | collective-permute-start | bytes 1572872 | tf_op jit(solution)/shard_map/ppermute | solution.py:40
  48.5 17.2 %collective-permute-start.14 = (bf16[64,4096]{1,0:T(8,128)(2,1)S(1)}, bf16[64,4096]{1,0:T(8,128)(2,1)S(1)}, u32[]{:S(2)}, u32[]{:S(2)}) collective-permute-start(bf16[64,4096]{1,0:T(8,128)(2,1)S(1)} %maximum_bitcast_fusion.1.refs_0_), channel_id=1, source_target_pairs={{0,48},{1,49},{2,50},{3,51},{4,52},{5,53},{6,54},{7,55},{8,56},{9,... | collective-permute-start | bytes 1572872 | tf_op jit(solution)/shard_map/ppermute | solution.py:40
  53.4 15.8 %collective-permute-start.12 = (bf16[64,4096]{1,0:T(8,128)(2,1)S(1)}, bf16[64,4096]{1,0:T(8,128)(2,1)S(1)}, u32[]{:S(2)}, u32[]{:S(2)}) collective-permute-start(bf16[64,4096]{1,0:T(8,128)(2,1)S(1)} %maximum_bitcast_fusion.1.refs_0_), channel_id=1, source_target_pairs={{0,16},{1,17},{2,18},{3,19},{4,20},{5,21},{6,22},{7,23},{8,24},{9,... | collective-permute-start | bytes 1572872 | tf_op jit(solution)/shard_map/ppermute | solution.py:40
  53.4 16.9 %collective-permute-start.16 = (bf16[64,4096]{1,0:T(8,128)(2,1)S(1)}, bf16[64,4096]{1,0:T(8,128)(2,1)}, u32[]{:S(2)}, u32[]{:S(2)}) collective-permute-start(bf16[64,4096]{1,0:T(8,128)(2,1)S(1)} %maximum_bitcast_fusion.1.refs_0_), channel_id=1, source_target_pairs={{0,65},{1,64},{2,67},{3,66},{4,69},{5,68},{6,71},{7,70},{8,73},{9,... | collective-permute-start | bytes 1572872 | tf_op jit(solution)/shard_map/ppermute | solution.py:40
  70.3 25.2 %collective-permute-start.18 = (bf16[128,4096]{1,0:T(8,128)(2,1)}, bf16[128,4096]{1,0:T(8,128)(2,1)}, u32[]{:S(2)}, u32[]{:S(2)}) collective-permute-start(bf16[128,4096]{1,0:T(8,128)(2,1)} %pad_maximum_fusion), channel_id=1, source_target_pairs={{0,65},{1,64},{2,67},{3,66},{4,69},{5,68},{6,71},{7,70},{8,73},{9,... | collective-permute-start | bytes 3145736 | tf_op jit(solution)/shard_map/ppermute | solution.py:40
  70.3 21.1 %collective-permute-start.17 = (bf16[64,4096]{1,0:T(8,128)(2,1)}, bf16[64,4096]{1,0:T(8,128)(2,1)}, u32[]{:S(2)}, u32[]{:S(2)}) collective-permute-start(bf16[64,4096]{1,0:T(8,128)(2,1)} %collective-permute-done.16.refs_3_), channel_id=1, source_target_pairs={{0,32},{1,33},{2,34},{3,35},{4,36},{5,37},{6,38},{7,39},{8,40},{9,... | collective-permute-start | bytes 1572872 | tf_op jit(solution)/shard_map/ppermute | solution.py:40
  71.1 18.2 %collective-permute-start.15 = (bf16[32,4096]{1,0:T(8,128)(2,1)}, bf16[32,4096]{1,0:T(8,128)(2,1)S(1)}, u32[]{:S(2)}, u32[]{:S(2)}) collective-permute-start(bf16[32,4096]{1,0:T(8,128)(2,1)} %slice.53), channel_id=1, source_target_pairs={{0,48},{1,49},{2,50},{3,51},{4,52},{5,53},{6,54},{7,55},{8,56},{9,... | collective-permute-start | bytes 786440 | tf_op jit(solution)/shard_map/ppermute | solution.py:40
  73.5 18.0 %collective-permute-start.13 = (bf16[32,4096]{1,0:T(8,128)(2,1)}, bf16[32,4096]{1,0:T(8,128)(2,1)}, u32[]{:S(2)}, u32[]{:S(2)}) collective-permute-start(bf16[32,4096]{1,0:T(8,128)(2,1)} %slice.52), channel_id=1, source_target_pairs={{0,16},{1,17},{2,18},{3,19},{4,20},{5,21},{6,22},{7,23},{8,24},{9,... | collective-permute-start | bytes 786440 | tf_op jit(solution)/shard_map/ppermute | solution.py:40
  110.2 14.9 %collective-permute-start.24 = (bf16[1024,256]{1,0:T(8,128)(2,1)}, bf16[1024,256]{1,0:T(8,128)(2,1)S(1)}, u32[]{:S(2)}, u32[]{:S(2)}) collective-permute-start(bf16[1024,256]{1,0:T(8,128)(2,1)} %pad_maximum_fusion.1), channel_id=1, source_target_pairs={{0,65},{1,64},{2,67},{3,66},{4,69},{5,68},{6,71},{7,70},{8,73},{9,... | collective-permute-start | bytes 1572872 | tf_op jit(solution)/shard_map/ppermute | solution.py:40
  111.8 13.4 %collective-permute-start.23 = (bf16[512,256]{1,0:T(8,128)(2,1)S(1)}, bf16[512,256]{1,0:T(8,128)(2,1)}, u32[]{:S(2)}, u32[]{:S(2)}) collective-permute-start(bf16[512,256]{1,0:T(8,128)(2,1)S(1)} %collective-permute-done.21.refs_3_), channel_id=1, source_target_pairs={{0,32},{1,33},{2,34},{3,35},{4,36},{5,37},{6,38},{7,39},{8,40},{9,... | collective-permute-start | bytes 786440 | tf_op jit(solution)/shard_map/ppermute | solution.py:40
  139.2 13.0 %collective-permute-start.26 = (bf16[128,2048]{1,0:T(8,128)(2,1)}, bf16[128,2048]{1,0:T(8,128)(2,1)S(1)}, u32[]{:S(2)}, u32[]{:S(2)}) collective-permute-start(bf16[128,2048]{1,0:T(8,128)(2,1)} %get-tuple-element.71), channel_id=1, source_target_pairs={{0,32},{1,33},{2,34},{3,35},{4,36},{5,37},{6,38},{7,39},{8,40},{9,... | collective-permute-start | bytes 1572872 | tf_op jit(solution)/shard_map/ppermute | solution.py:40
  139.9 14.2 %collective-permute-start.27 = (bf16[128,2048]{1,0:T(8,128)(2,1)}, bf16[128,2048]{1,0:T(8,128)(2,1)S(1)}, u32[]{:S(2)}, u32[]{:S(2)}) collective-permute-start(bf16[128,2048]{1,0:T(8,128)(2,1)} %get-tuple-element.73), channel_id=1, source_target_pairs={{0,65},{1,64},{2,67},{3,66},{4,69},{5,68},{6,71},{7,70},{8,73},{9,... | collective-permute-start | bytes 1572872 | tf_op jit(solution)/shard_map/ppermute | solution.py:40
  165.6 13.2 %collective-permute-start.31 = (bf16[64,2048]{1,0:T(8,128)(2,1)S(1)}, bf16[64,2048]{1,0:T(8,128)(2,1)S(1)}, u32[]{:S(2)}, u32[]{:S(2)}) collective-permute-start(bf16[64,2048]{1,0:T(8,128)(2,1)S(1)} %join_sums.2.refs_0_.refs_5_), channel_id=1, source_target_pairs={{0,16},{1,17},{2,18},{3,19},{4,20},{5,21},{6,22},{7,23},{8,24},{9,... | collective-permute-start | bytes 786440 | tf_op jit(solution)/shard_map/ppermute | solution.py:40
  167.5 12.3 %collective-permute-start.33 = (bf16[64,2048]{1,0:T(8,128)(2,1)S(1)}, bf16[64,2048]{1,0:T(8,128)(2,1)S(1)}, u32[]{:S(2)}, u32[]{:S(2)}) collective-permute-start(bf16[64,2048]{1,0:T(8,128)(2,1)S(1)} %join_sums.2.refs_0_.refs_5_), channel_id=1, source_target_pairs={{0,65},{1,64},{2,67},{3,66},{4,69},{5,68},{6,71},{7,70},{8,73},{9,... | collective-permute-start | bytes 786440 | tf_op jit(solution)/shard_map/ppermute | solution.py:40
  178.9 16.4 %collective-permute-start.36 = (bf16[128,2048]{1,0:T(8,128)(2,1)S(1)}, bf16[128,2048]{1,0:T(8,128)(2,1)S(1)}, u32[]{:S(2)}, u32[]{:S(2)}) collective-permute-start(bf16[128,2048]{1,0:T(8,128)(2,1)S(1)} %pad_maximum_fusion.2), channel_id=1, source_target_pairs={{0,65},{1,64},{2,67},{3,66},{4,69},{5,68},{6,71},{7,70},{8,73},{9,... | collective-permute-start | bytes 1572872 | tf_op jit(solution)/shard_map/ppermute | solution.py:40
  179.9 15.4 %collective-permute-start.35 = (bf16[64,2048]{1,0:T(8,128)(2,1)S(1)}, bf16[64,2048]{1,0:T(8,128)(2,1)S(1)}, u32[]{:S(2)}, u32[]{:S(2)}) collective-permute-start(bf16[64,2048]{1,0:T(8,128)(2,1)S(1)} %collective-permute-done.33.refs_3_), channel_id=1, source_target_pairs={{0,32},{1,33},{2,34},{3,35},{4,36},{5,37},{6,38},{7,39},{8,40},{9,... | collective-permute-start | bytes 786440 | tf_op jit(solution)/shard_map/ppermute | solution.py:40
  199.1 11.7 %collective-permute-start.38 = (bf16[128,2048]{1,0:T(8,128)(2,1)S(1)}, bf16[128,2048]{1,0:T(8,128)(2,1)S(1)}, u32[]{:S(2)}, u32[]{:S(2)}) collective-permute-start(bf16[128,2048]{1,0:T(8,128)(2,1)S(1)} %get-tuple-element.82), channel_id=1, source_target_pairs={{0,65},{1,64},{2,67},{3,66},{4,69},{5,68},{6,71},{7,70},{8,73},{9,... | collective-permute-start | bytes 1572872 | tf_op jit(solution)/shard_map/ppermute | solution.py:40
  219.2 15.2 %collective-permute-start.42 = (bf16[64,2048]{1,0:T(8,128)(2,1)S(1)}, bf16[64,2048]{1,0:T(8,128)(2,1)S(1)}, u32[]{:S(2)}, u32[]{:S(2)}) collective-permute-start(bf16[64,2048]{1,0:T(8,128)(2,1)S(1)} %join_sums.3), channel_id=1, source_target_pairs={{0,0},{1,65},{2,2},{3,67},{4,4},{5,69},{6,6},{7,71},{8,16},{9,81},... | collective-permute-start | bytes 786440 | tf_op jit(solution)/shard_map/ppermute | solution.py:40
  (41 other events, 472.7 us)

commit v3 on v2

--- a/solution.py
+++ b/solution.py
@@ -301,14 +301,20 @@
 def merge_kernel(count, ahead, core_ref, *refs):
     pieces, refs = refs[:count], refs[count:]
     own_hbm, other_hbm, *done, out_ref, x, weight, arrived = refs
-    land(
-        fetch(
-            [(own_hbm, weight.at[:, :LANES]), (other_hbm, weight.at[:, LANES:])]
-            + rows_of(pieces, x),
-            arrived,
-        )
-    )
-    both = jnp.dot(x[...], weight[...], preferred_element_type=jnp.float32).astype(jnp.bfloat16)
+    step = x.shape[1] // 2
+    copies = []
+    for i in range(2):
+        cols = pl.ds(i * step, step)
+        pairs = [(own_hbm.at[cols, :], weight.at[cols, :LANES])]
+        pairs.append((other_hbm.at[cols, :], weight.at[cols, LANES:]))
+        pairs += [(piece.at[:, cols], part.at[:, cols]) for piece, part in rows_of(pieces, x)]
+        copies.append(fetch(pairs, arrived.at[i]))
+    both = jnp.zeros((x.shape[0], 2 * LANES), jnp.float32)
+    for i in range(2):
+        cols = slice(i * step, (i + 1) * step)
+        land(copies[i])
+        both = both + jnp.dot(x[:, cols], weight[cols, :], preferred_element_type=jnp.float32)
+    both = both.astype(jnp.bfloat16)
     own, other = both[:, :LANES], both[:, LANES:]
     first = core_ref[0] == 0
     if ahead:
@@ -332,7 +338,7 @@
         scratch_shapes=[
             pltpu.VMEM((tokens, pieces[0].shape[1]), jnp.bfloat16),
             pltpu.VMEM((own.shape[0], 2 * LANES), jnp.bfloat16),
-            pltpu.SemaphoreType.DMA((len(pieces) + 2,)),
+            pltpu.SemaphoreType.DMA((2, len(pieces) + 2)),
         ],
         compiler_params=pltpu.CompilerParams(vmem_limit_bytes=MOST - 3 * 1024 * 1024),
         name="merge_patches",

time: 235 us -> 235 us (level)
  no operation moved by 1% of the time
where the time goes in v3:
time: 235 us
  waiting for transfers between devices  115 us (49%)
  starting transfers between devices  54.7 us (23%)
  Pallas kernels  47.9 us (20%)
  other arithmetic  8.61 us (4%)
  local copies, waits for them, and re-layouts  8.56 us (4%)
    ppermute x43, waiting for transfers between devices, permute(): return lax.ppermute(value, ('row', 'col'), pairs)  115 us
    ppermute x43, starting transfers between devices, permute(): return lax.ppermute(value, ('row', 'col'), pairs)  54.7 us
    pallas_call x1, Pallas kernels, first_attention(): pl.pallas_call(first_kernel, in_specs=[vmem] * 4 + [anywhere, vmem, anywh...  18.2 us
    pallas_call x1, Pallas kernels, second_attention(): pl.pallas_call(second_kernel, in_specs=[smem] + [anywhere] * (PIECES + 2)...  13.2 us
    pallas_call x2, Pallas kernels, merge(): pl.pallas_call(functools.partial(merge_kernel, len(pieces), ahead), in_sp...  8.17 us
    pallas_call x2, Pallas kernels, feed_half(): pl.pallas_call(functools.partial(feed_kernel, len(pieces), takes), in_spe...  7.51 us
  transfers between devices with their start and end apart: 43, of which 26 were waited for; matrix products, arithmetic and copies ran while one was open for 6% of the time, Pallas kernels for 11%

profile of v3, /device:TPU:32, one launch (start us, length us, event | category | flops | bytes accessed | tf_op | source)
XLA Modules:
  0.0 234.9 jit_solution(729874501762676924)
XLA Ops:
  1.9 5.0 %collective-permute-start.1 = (bf16[8,8,1024]{2,1,0:T(8,128)(2,1)}, bf16[8,8,1024]{2,1,0:T(8,128)(2,1)S(1)}, u32[]{:S(2)}, u32[]{:S(2)}) collective-permute-start(bf16[8,8,1024]{2,1,0:T(8,128)(2,1)} %get-tuple-element.90), channel_id=1, source_target_pairs={{0,120},{1,121},{2,122},{3,123},{4,124},{5,125},{6,126},{7,127},{8... | collective-permute-start | bytes 393224 | tf_op jit(solution)/shard_map/ppermute | solution.py:40
  6.9 3.3 %collective-permute-start = (bf16[8,8,1024]{2,1,0:T(8,128)(2,1)}, bf16[8,8,1024]{2,1,0:T(8,128)(2,1)S(1)}, u32[]{:S(2)}, u32[]{:S(2)}) collective-permute-start(bf16[8,8,1024]{2,1,0:T(8,128)(2,1)} %get-tuple-element.91), channel_id=1, source_target_pairs={{0,127},{1,120},{2,121},{3,122},{4,123},{5,124},{6,125},{7,126},{8... | collective-permute-start | bytes 393224 | tf_op jit(solution)/shard_map/ppermute | solution.py:40
  17.4 18.2 %first_attention.1 = (bf16[16,4096]{1,0:T(8,128)(2,1)}, bf16[16,4096]{1,0:T(8,128)(2,1)}, bf16[16,4096]{1,0:T(8,128)(2,1)}, bf16[16,4096]{1,0:T(8,128)(2,1)}) custom-call(bf16[64,1024]{1,0:T(8,128)(2,1)} %get-tuple-element.48.refs_0_, bf16[64,1024]{1,0:T(8,128)(2,1)} %bitcast.43, bf16[64,1024]{1,0:T(8,128)(2,1)} %bitcast.42, bf16[64,1024]{1,0:T(8,128)(2,1)} %bitcast.44, ...), custom_call_target="tpu_custom_call" | custom-call | tf_op jit(solution)/shard_map/first_attention/pallas_call | solution.py:245
  48.5 4.9 %collective-permute-start.14 = (bf16[64,4096]{1,0:T(8,128)(2,1)S(1)}, bf16[64,4096]{1,0:T(8,128)(2,1)S(1)}, u32[]{:S(2)}, u32[]{:S(2)}) collective-permute-start(bf16[64,4096]{1,0:T(8,128)(2,1)S(1)} %maximum_bitcast_fusion.1.refs_0_), channel_id=1, source_target_pairs={{0,48},{1,49},{2,50},{3,51},{4,52},{5,53},{6,54},{7,55},{8,56},{9,... | collective-permute-start | bytes 1572872 | tf_op jit(solution)/shard_map/ppermute | solution.py:40
  53.4 12.3 %collective-permute-done.14.refs_2_ = bf16[64,4096]{1,0:T(8,128)(2,1)S(1)} collective-permute-done((bf16[64,4096]{1,0:T(8,128)(2,1)S(1)}, bf16[64,4096]{1,0:T(8,128)(2,1)S(1)}, u32[]{:S(2)}, u32[]{:S(2)}) %collective-permute-start.14) | collective-permute-done | bytes 524320 | tf_op jit(solution)/shard_map/ppermute | solution.py:40
  65.7 3.5 %collective-permute-done.12.refs_1_ = bf16[64,4096]{1,0:T(8,128)(2,1)S(1)} collective-permute-done((bf16[64,4096]{1,0:T(8,128)(2,1)S(1)}, bf16[64,4096]{1,0:T(8,128)(2,1)S(1)}, u32[]{:S(2)}, u32[]{:S(2)}) %collective-permute-start.12) | collective-permute-done | bytes 524320 | tf_op jit(solution)/shard_map/ppermute | solution.py:40
  73.8 3.6 %merge_patches.2.refs_6_ = bf16[256,256]{1,0:T(8,128)(2,1)} custom-call(s32[1]{0:T(128)} %bitcast.core_ref, bf16[64,4096]{1,0:T(8,128)(2,1)} %copy-done.8, bf16[64,4096]{1,0:T(8,128)(2,1)} %copy-done.7, bf16[64,4096]{1,0:T(8,128)(2,1)} %copy-done.6, bf16[64,4096]{1,0:T(8,128)(2,1)} %collective-permute-done.16.refs_3_, bf16[4096,128]{1,0:T(8,128)(2,1)} %refs_4_.3, ...), custom_call_target="tpu_custom_call" | custom-call | tf_op jit(solution)/shard_map/merge_patches/pallas_call | solution.py:331
  77.5 11.8 %collective-permute-done.15.refs_1_ = bf16[32,4096]{1,0:T(8,128)(2,1)S(1)} collective-permute-done((bf16[32,4096]{1,0:T(8,128)(2,1)}, bf16[32,4096]{1,0:T(8,128)(2,1)S(1)}, u32[]{:S(2)}, u32[]{:S(2)}) %collective-permute-start.15) | collective-permute-done | bytes 262176 | tf_op jit(solution)/shard_map/ppermute | solution.py:40
  91.5 4.1 %collective-permute-done.18.refs_3_ = bf16[128,4096]{1,0:T(8,128)(2,1)} collective-permute-done((bf16[128,4096]{1,0:T(8,128)(2,1)}, bf16[128,4096]{1,0:T(8,128)(2,1)}, u32[]{:S(2)}, u32[]{:S(2)}) %collective-permute-start.18) | collective-permute-done | bytes 1048608 | tf_op jit(solution)/shard_map/ppermute | solution.py:40
  95.6 4.6 %merge_patches.3.refs_0_ = bf16[512,256]{1,0:T(8,128)(2,1)} custom-call(s32[1]{0:T(128)} %bitcast.core_ref, bf16[32,4096]{1,0:T(8,128)(2,1)} %collective-permute-done.13.refs_0_, bf16[32,4096]{1,0:T(8,128)(2,1)} %copy-done.14, bf16[64,4096]{1,0:T(8,128)(2,1)} %collective-permute-done.17.refs_2_, bf16[128,4096]{1,0:T(8,128)(2,1)} %collective-permute-done.18.refs_3_, ...), custom_call_target="tpu_custom_call" | custom-call | tf_op jit(solution)/shard_map/merge_patches/pallas_call | solution.py:331
  102.9 4.7 %collective-permute-done.20.refs_2_ = bf16[512,256]{1,0:T(8,128)(2,1)S(1)} collective-permute-done((bf16[512,256]{1,0:T(8,128)(2,1)}, bf16[512,256]{1,0:T(8,128)(2,1)S(1)}, u32[]{:S(2)}, u32[]{:S(2)}) %collective-permute-start.20) | collective-permute-done | bytes 262176 | tf_op jit(solution)/shard_map/ppermute | solution.py:40
  116.9 5.4 %collective-permute-done.22.refs_4_ = bf16[512,256]{1,0:T(8,128)(2,1)} collective-permute-done((bf16[512,256]{1,0:T(8,128)(2,1)}, bf16[512,256]{1,0:T(8,128)(2,1)}, u32[]{:S(2)}, u32[]{:S(2)}) %collective-permute-start.22) | collective-permute-done | bytes 262176 | tf_op jit(solution)/shard_map/ppermute | solution.py:40
  126.0 13.2 %second_attention.1 = (bf16[64,2048]{1,0:T(8,128)(2,1)}, bf16[64,2048]{1,0:T(8,128)(2,1)}, bf16[64,2048]{1,0:T(8,128)(2,1)}, bf16[64,2048]{1,0:T(8,128)(2,1)}, b...) custom-call(s32[16]{0:T(128)} %pad_add_fusion.at_ref, ...), custom_call_target="tpu_custom_call" | custom-call | tf_op jit(solution)/shard_map/second_attention/pallas_call | solution.py:410
  140.8 11.2 %collective-permute-done.26.refs_1_ = bf16[128,2048]{1,0:T(8,128)(2,1)S(1)} collective-permute-done((bf16[128,2048]{1,0:T(8,128)(2,1)}, bf16[128,2048]{1,0:T(8,128)(2,1)S(1)}, u32[]{:S(2)}, u32[]{:S(2)}) %collective-permute-start.26) | collective-permute-done | bytes 524320 | tf_op jit(solution)/shard_map/ppermute | solution.py:40
  168.3 6.1 %collective-permute-done.32.refs_2_ = bf16[64,2048]{1,0:T(8,128)(2,1)S(1)} collective-permute-done((bf16[64,2048]{1,0:T(8,128)(2,1)S(1)}, bf16[64,2048]{1,0:T(8,128)(2,1)S(1)}, u32[]{:S(2)}, u32[]{:S(2)}) %collective-permute-start.32) | collective-permute-done | bytes 262176 | tf_op jit(solution)/shard_map/ppermute | solution.py:40
  174.4 4.2 %collective-permute-done.31.refs_1_ = bf16[64,2048]{1,0:T(8,128)(2,1)S(1)} collective-permute-done((bf16[64,2048]{1,0:T(8,128)(2,1)S(1)}, bf16[64,2048]{1,0:T(8,128)(2,1)S(1)}, u32[]{:S(2)}, u32[]{:S(2)}) %collective-permute-start.31) | collective-permute-done | bytes 262176 | tf_op jit(solution)/shard_map/ppermute | solution.py:40
  179.7 3.5 %collective-permute-start.35 = (bf16[64,2048]{1,0:T(8,128)(2,1)S(1)}, bf16[64,2048]{1,0:T(8,128)(2,1)S(1)}, u32[]{:S(2)}, u32[]{:S(2)}) collective-permute-start(bf16[64,2048]{1,0:T(8,128)(2,1)S(1)} %collective-permute-done.33.refs_3_), channel_id=1, source_target_pairs={{0,32},{1,33},{2,34},{3,35},{4,36},{5,37},{6,38},{7,39},{8,40},{9,... | collective-permute-start | bytes 786440 | tf_op jit(solution)/shard_map/ppermute | solution.py:40
  183.2 6.3 %collective-permute-done.34.refs_0_ = bf16[64,2048]{1,0:T(8,128)(2,1)S(1)} collective-permute-done((bf16[64,2048]{1,0:T(8,128)(2,1)S(1)}, bf16[64,2048]{1,0:T(8,128)(2,1)S(1)}, u32[]{:S(2)}, u32[]{:S(2)}) %collective-permute-start.34) | collective-permute-done | bytes 262176 | tf_op jit(solution)/shard_map/ppermute | solution.py:40
  189.5 5.6 %collective-permute-done.35.refs_1_ = bf16[64,2048]{1,0:T(8,128)(2,1)S(1)} collective-permute-done((bf16[64,2048]{1,0:T(8,128)(2,1)S(1)}, bf16[64,2048]{1,0:T(8,128)(2,1)S(1)}, u32[]{:S(2)}, u32[]{:S(2)}) %collective-permute-start.35) | collective-permute-done | bytes 262176 | tf_op jit(solution)/shard_map/ppermute | solution.py:40
  195.1 3.8 %feed_forward.3 = (bf16[128,2048]{1,0:T(8,128)(2,1)S(1)}, bf16[128,2048]{1,0:T(8,128)(2,1)S(1)}) custom-call(bf16[64,2048]{1,0:T(8,128)(2,1)S(1)} %collective-permute-done.34.refs_0_, bf16[64,2048]{1,0:T(8,128)(2,1)S(1)} %collective-permute-done.35.refs_1_, bf16[128,2048]{1,0:T(8,128)(2,1)S(1)} %collective-permute-done.36.refs_2_, ...), custom_call_target="tpu_custom_call" | custom-call | tf_op jit(solution)/shard_map/feed_forward/pallas_call | solution.py:465
  199.9 3.8 %feed_forward.2 = (bf16[64,2048]{1,0:T(8,128)(2,1)S(1)}, bf16[64,2048]{1,0:T(8,128)(2,1)S(1)}, bf16[64,2048]{1,0:T(8,128)(2,1)S(1)}, bf16[64,2048]{1,0:T(8,128)(2,1)S(1)}) custom-call(bf16[64,2048]{1,0:T(8,128)(2,1)S(1)} %join_sums.2.refs_0_.refs_5_, bf16[64,2048]{1,0:T(8,128)(2,1)S(1)} %collective-permute-done.31.refs_1_, ...), custom_call_target="tpu_custom_call" | custom-call | tf_op jit(solution)/shard_map/feed_forward/pallas_call | solution.py:465
  203.7 5.9 %collective-permute-done.37.refs_1_ = bf16[128,2048]{1,0:T(8,128)(2,1)S(1)} collective-permute-done((bf16[128,2048]{1,0:T(8,128)(2,1)S(1)}, bf16[128,2048]{1,0:T(8,128)(2,1)S(1)}, u32[]{:S(2)}, u32[]{:S(2)}) %collective-permute-start.37) | collective-permute-done | bytes 524320 | tf_op jit(solution)/shard_map/ppermute | solution.py:40
  219.0 8.2 %collective-permute-start.42 = (bf16[64,2048]{1,0:T(8,128)(2,1)S(1)}, bf16[64,2048]{1,0:T(8,128)(2,1)S(1)}, u32[]{:S(2)}, u32[]{:S(2)}) collective-permute-start(bf16[64,2048]{1,0:T(8,128)(2,1)S(1)} %join_sums.3), channel_id=1, source_target_pairs={{0,0},{1,65},{2,2},{3,67},{4,4},{5,69},{6,6},{7,71},{8,16},{9,81},... | collective-permute-start | bytes 786440 | tf_op jit(solution)/shard_map/ppermute | solution.py:40
  227.2 6.9 %collective-permute-done.42 = bf16[64,2048]{1,0:T(8,128)(2,1)S(1)} collective-permute-done((bf16[64,2048]{1,0:T(8,128)(2,1)S(1)}, bf16[64,2048]{1,0:T(8,128)(2,1)S(1)}, u32[]{:S(2)}, u32[]{:S(2)}) %collective-permute-start.42) | collective-permute-done | bytes 262176 | tf_op jit(solution)/shard_map/ppermute | solution.py:40
  (153 shorter events, 74.1 us)
Async XLA Ops:
  1.9 13.1 %collective-permute-start.2 = (bf16[8,8,1024]{2,1,0:T(8,128)(2,1)}, bf16[8,8,1024]{2,1,0:T(8,128)(2,1)S(1)}, u32[]{:S(2)}, u32[]{:S(2)}) collective-permute-start(bf16[8,8,1024]{2,1,0:T(8,128)(2,1)} %get-tuple-element.89), channel_id=1, source_target_pairs={{0,7},{1,0},{2,1},{3,2},{4,3},{5,4},{6,5},{7,6},{8,15},{9,8},{10,9... | collective-permute-start | bytes 393224 | tf_op jit(solution)/shard_map/ppermute | solution.py:40
  1.9 13.0 %collective-permute-start.1 = (bf16[8,8,1024]{2,1,0:T(8,128)(2,1)}, bf16[8,8,1024]{2,1,0:T(8,128)(2,1)S(1)}, u32[]{:S(2)}, u32[]{:S(2)}) collective-permute-start(bf16[8,8,1024]{2,1,0:T(8,128)(2,1)} %get-tuple-element.90), channel_id=1, source_target_pairs={{0,120},{1,121},{2,122},{3,123},{4,124},{5,125},{6,126},{7,127},{8... | collective-permute-start | bytes 393224 | tf_op jit(solution)/shard_map/ppermute | solution.py:40
  15.0 20.6 %collective-permute-start.6 = (bf16[2048,512]{1,0:T(8,128)(2,1)S(1)}, bf16[2048,512]{1,0:T(8,128)(2,1)}, u32[]{:S(2)}, u32[]{:S(2)}) collective-permute-start(bf16[2048,512]{1,0:T(8,128)(2,1)S(1)} %copy-done), channel_id=1, source_target_pairs={{0,8},{1,9},{2,10},{3,11},{4,12},{5,13},{6,14},{7,15},{8,0},{9,1},... | collective-permute-start | bytes 6291464 | tf_op jit(solution)/shard_map/ppermute | solution.py:40
  16.3 19.3 %collective-permute-start.7 = (bf16[512,2048]{1,0:T(8,128)(2,1)}, bf16[512,2048]{1,0:T(8,128)(2,1)}, u32[]{:S(2)}, u32[]{:S(2)}) collective-permute-start(bf16[512,2048]{1,0:T(8,128)(2,1)} %refs_5_), channel_id=1, source_target_pairs={{0,8},{1,9},{2,10},{3,11},{4,12},{5,13},{6,14},{7,15},{8,0},{9,1},... | collective-permute-start | bytes 6291464 | tf_op jit(solution)/shard_map/ppermute | solution.py:40
  16.4 19.2 %collective-permute-start.4 = (bf16[3,2048,128]{2,1,0:T(8,128)(2,1)}, bf16[3,2048,128]{2,1,0:T(8,128)(2,1)}, u32[]{:S(2)}, u32[]{:S(2)}) collective-permute-start(bf16[3,2048,128]{2,1,0:T(8,128)(2,1)} %refs_7_), channel_id=1, source_target_pairs={{0,8},{1,9},{2,10},{3,11},{4,12},{5,13},{6,14},{7,15},{8,0},{9,1},... | collective-permute-start | bytes 4718600 | tf_op jit(solution)/shard_map/ppermute | solution.py:40
  16.8 18.8 %collective-permute-start.3 = (bf16[4096,128]{1,0:T(8,128)(2,1)}, bf16[4096,128]{1,0:T(8,128)(2,1)}, u32[]{:S(2)}, u32[]{:S(2)}) collective-permute-start(bf16[4096,128]{1,0:T(8,128)(2,1)} %refs_4_.3), channel_id=1, source_target_pairs={{0,8},{1,9},{2,10},{3,11},{4,12},{5,13},{6,14},{7,15},{8,0},{9,1},... | collective-permute-start | bytes 3145736 | tf_op jit(solution)/shard_map/ppermute | solution.py:40
  16.9 18.7 %collective-permute-start.5 = (bf16[128,2048]{1,0:T(8,128)(2,1)}, bf16[128,2048]{1,0:T(8,128)(2,1)S(1)}, u32[]{:S(2)}, u32[]{:S(2)}) collective-permute-start(bf16[128,2048]{1,0:T(8,128)(2,1)} %refs_11_), channel_id=1, source_target_pairs={{0,8},{1,9},{2,10},{3,11},{4,12},{5,13},{6,14},{7,15},{8,0},{9,1},... | collective-permute-start | bytes 1572872 | tf_op jit(solution)/shard_map/ppermute | solution.py:40
  48.5 17.2 %collective-permute-start.14 = (bf16[64,4096]{1,0:T(8,128)(2,1)S(1)}, bf16[64,4096]{1,0:T(8,128)(2,1)S(1)}, u32[]{:S(2)}, u32[]{:S(2)}) collective-permute-start(bf16[64,4096]{1,0:T(8,128)(2,1)S(1)} %maximum_bitcast_fusion.1.refs_0_), channel_id=1, source_target_pairs={{0,48},{1,49},{2,50},{3,51},{4,52},{5,53},{6,54},{7,55},{8,56},{9,... | collective-permute-start | bytes 1572872 | tf_op jit(solution)/shard_map/ppermute | solution.py:40
  53.4 15.8 %collective-permute-start.12 = (bf16[64,4096]{1,0:T(8,128)(2,1)S(1)}, bf16[64,4096]{1,0:T(8,128)(2,1)S(1)}, u32[]{:S(2)}, u32[]{:S(2)}) collective-permute-start(bf16[64,4096]{1,0:T(8,128)(2,1)S(1)} %maximum_bitcast_fusion.1.refs_0_), channel_id=1, source_target_pairs={{0,16},{1,17},{2,18},{3,19},{4,20},{5,21},{6,22},{7,23},{8,24},{9,... | collective-permute-start | bytes 1572872 | tf_op jit(solution)/shard_map/ppermute | solution.py:40
  53.4 16.9 %collective-permute-start.16 = (bf16[64,4096]{1,0:T(8,128)(2,1)S(1)}, bf16[64,4096]{1,0:T(8,128)(2,1)}, u32[]{:S(2)}, u32[]{:S(2)}) collective-permute-start(bf16[64,4096]{1,0:T(8,128)(2,1)S(1)} %maximum_bitcast_fusion.1.refs_0_), channel_id=1, source_target_pairs={{0,65},{1,64},{2,67},{3,66},{4,69},{5,68},{6,71},{7,70},{8,73},{9,... | collective-permute-start | bytes 1572872 | tf_op jit(solution)/shard_map/ppermute | solution.py:40
  70.3 25.2 %collective-permute-start.18 = (bf16[128,4096]{1,0:T(8,128)(2,1)}, bf16[128,4096]{1,0:T(8,128)(2,1)}, u32[]{:S(2)}, u32[]{:S(2)}) collective-permute-start(bf16[128,4096]{1,0:T(8,128)(2,1)} %pad_maximum_fusion), channel_id=1, source_target_pairs={{0,65},{1,64},{2,67},{3,66},{4,69},{5,68},{6,71},{7,70},{8,73},{9,... | collective-permute-start | bytes 3145736 | tf_op jit(solution)/shard_map/ppermute | solution.py:40
  70.3 21.1 %collective-permute-start.17 = (bf16[64,4096]{1,0:T(8,128)(2,1)}, bf16[64,4096]{1,0:T(8,128)(2,1)}, u32[]{:S(2)}, u32[]{:S(2)}) collective-permute-start(bf16[64,4096]{1,0:T(8,128)(2,1)} %collective-permute-done.16.refs_3_), channel_id=1, source_target_pairs={{0,32},{1,33},{2,34},{3,35},{4,36},{5,37},{6,38},{7,39},{8,40},{9,... | collective-permute-start | bytes 1572872 | tf_op jit(solution)/shard_map/ppermute | solution.py:40
  71.1 18.2 %collective-permute-start.15 = (bf16[32,4096]{1,0:T(8,128)(2,1)}, bf16[32,4096]{1,0:T(8,128)(2,1)S(1)}, u32[]{:S(2)}, u32[]{:S(2)}) collective-permute-start(bf16[32,4096]{1,0:T(8,128)(2,1)} %slice.53), channel_id=1, source_target_pairs={{0,48},{1,49},{2,50},{3,51},{4,52},{5,53},{6,54},{7,55},{8,56},{9,... | collective-permute-start | bytes 786440 | tf_op jit(solution)/shard_map/ppermute | solution.py:40
  73.5 18.0 %collective-permute-start.13 = (bf16[32,4096]{1,0:T(8,128)(2,1)}, bf16[32,4096]{1,0:T(8,128)(2,1)}, u32[]{:S(2)}, u32[]{:S(2)}) collective-permute-start(bf16[32,4096]{1,0:T(8,128)(2,1)} %slice.52), channel_id=1, source_target_pairs={{0,16},{1,17},{2,18},{3,19},{4,20},{5,21},{6,22},{7,23},{8,24},{9,... | collective-permute-start | bytes 786440 | tf_op jit(solution)/shard_map/ppermute | solution.py:40
  110.3 14.9 %collective-permute-start.24 = (bf16[1024,256]{1,0:T(8,128)(2,1)}, bf16[1024,256]{1,0:T(8,128)(2,1)S(1)}, u32[]{:S(2)}, u32[]{:S(2)}) collective-permute-start(bf16[1024,256]{1,0:T(8,128)(2,1)} %pad_maximum_fusion.1), channel_id=1, source_target_pairs={{0,65},{1,64},{2,67},{3,66},{4,69},{5,68},{6,71},{7,70},{8,73},{9,... | collective-permute-start | bytes 1572872 | tf_op jit(solution)/shard_map/ppermute | solution.py:40
  111.8 13.4 %collective-permute-start.23 = (bf16[512,256]{1,0:T(8,128)(2,1)S(1)}, bf16[512,256]{1,0:T(8,128)(2,1)}, u32[]{:S(2)}, u32[]{:S(2)}) collective-permute-start(bf16[512,256]{1,0:T(8,128)(2,1)S(1)} %collective-permute-done.21.refs_3_), channel_id=1, source_target_pairs={{0,32},{1,33},{2,34},{3,35},{4,36},{5,37},{6,38},{7,39},{8,40},{9,... | collective-permute-start | bytes 786440 | tf_op jit(solution)/shard_map/ppermute | solution.py:40
  139.3 12.8 %collective-permute-start.26 = (bf16[128,2048]{1,0:T(8,128)(2,1)}, bf16[128,2048]{1,0:T(8,128)(2,1)S(1)}, u32[]{:S(2)}, u32[]{:S(2)}) collective-permute-start(bf16[128,2048]{1,0:T(8,128)(2,1)} %get-tuple-element.71), channel_id=1, source_target_pairs={{0,32},{1,33},{2,34},{3,35},{4,36},{5,37},{6,38},{7,39},{8,40},{9,... | collective-permute-start | bytes 1572872 | tf_op jit(solution)/shard_map/ppermute | solution.py:40
  139.7 14.2 %collective-permute-start.27 = (bf16[128,2048]{1,0:T(8,128)(2,1)}, bf16[128,2048]{1,0:T(8,128)(2,1)S(1)}, u32[]{:S(2)}, u32[]{:S(2)}) collective-permute-start(bf16[128,2048]{1,0:T(8,128)(2,1)} %get-tuple-element.73), channel_id=1, source_target_pairs={{0,65},{1,64},{2,67},{3,66},{4,69},{5,68},{6,71},{7,70},{8,73},{9,... | collective-permute-start | bytes 1572872 | tf_op jit(solution)/shard_map/ppermute | solution.py:40
  165.4 13.2 %collective-permute-start.31 = (bf16[64,2048]{1,0:T(8,128)(2,1)S(1)}, bf16[64,2048]{1,0:T(8,128)(2,1)S(1)}, u32[]{:S(2)}, u32[]{:S(2)}) collective-permute-start(bf16[64,2048]{1,0:T(8,128)(2,1)S(1)} %join_sums.2.refs_0_.refs_5_), channel_id=1, source_target_pairs={{0,16},{1,17},{2,18},{3,19},{4,20},{5,21},{6,22},{7,23},{8,24},{9,... | collective-permute-start | bytes 786440 | tf_op jit(solution)/shard_map/ppermute | solution.py:40
  167.3 12.3 %collective-permute-start.33 = (bf16[64,2048]{1,0:T(8,128)(2,1)S(1)}, bf16[64,2048]{1,0:T(8,128)(2,1)S(1)}, u32[]{:S(2)}, u32[]{:S(2)}) collective-permute-start(bf16[64,2048]{1,0:T(8,128)(2,1)S(1)} %join_sums.2.refs_0_.refs_5_), channel_id=1, source_target_pairs={{0,65},{1,64},{2,67},{3,66},{4,69},{5,68},{6,71},{7,70},{8,73},{9,... | collective-permute-start | bytes 786440 | tf_op jit(solution)/shard_map/ppermute | solution.py:40
  178.6 16.4 %collective-permute-start.36 = (bf16[128,2048]{1,0:T(8,128)(2,1)S(1)}, bf16[128,2048]{1,0:T(8,128)(2,1)S(1)}, u32[]{:S(2)}, u32[]{:S(2)}) collective-permute-start(bf16[128,2048]{1,0:T(8,128)(2,1)S(1)} %pad_maximum_fusion.2), channel_id=1, source_target_pairs={{0,65},{1,64},{2,67},{3,66},{4,69},{5,68},{6,71},{7,70},{8,73},{9,... | collective-permute-start | bytes 1572872 | tf_op jit(solution)/shard_map/ppermute | solution.py:40
  179.7 15.4 %collective-permute-start.35 = (bf16[64,2048]{1,0:T(8,128)(2,1)S(1)}, bf16[64,2048]{1,0:T(8,128)(2,1)S(1)}, u32[]{:S(2)}, u32[]{:S(2)}) collective-permute-start(bf16[64,2048]{1,0:T(8,128)(2,1)S(1)} %collective-permute-done.33.refs_3_), channel_id=1, source_target_pairs={{0,32},{1,33},{2,34},{3,35},{4,36},{5,37},{6,38},{7,39},{8,40},{9,... | collective-permute-start | bytes 786440 | tf_op jit(solution)/shard_map/ppermute | solution.py:40
  199.0 11.7 %collective-permute-start.38 = (bf16[128,2048]{1,0:T(8,128)(2,1)S(1)}, bf16[128,2048]{1,0:T(8,128)(2,1)S(1)}, u32[]{:S(2)}, u32[]{:S(2)}) collective-permute-start(bf16[128,2048]{1,0:T(8,128)(2,1)S(1)} %get-tuple-element.82), channel_id=1, source_target_pairs={{0,65},{1,64},{2,67},{3,66},{4,69},{5,68},{6,71},{7,70},{8,73},{9,... | collective-permute-start | bytes 1572872 | tf_op jit(solution)/shard_map/ppermute | solution.py:40
  219.0 15.2 %collective-permute-start.42 = (bf16[64,2048]{1,0:T(8,128)(2,1)S(1)}, bf16[64,2048]{1,0:T(8,128)(2,1)S(1)}, u32[]{:S(2)}, u32[]{:S(2)}) collective-permute-start(bf16[64,2048]{1,0:T(8,128)(2,1)S(1)} %join_sums.3), channel_id=1, source_target_pairs={{0,0},{1,65},{2,2},{3,67},{4,4},{5,69},{6,6},{7,71},{8,16},{9,81},... | collective-permute-start | bytes 786440 | tf_op jit(solution)/shard_map/ppermute | solution.py:40
  (41 other events, 472.1 us)
